TPU v7x, 256 devices: a whole 4x4x8 slice. The times are simulated.
256 devices in a mesh: blk: 64 (over x, z, core), op: 4 (over y).
Axes of the slice: x: 4, y: 4, z: 8, core: 2. Of those that a mesh axis runs over, the one named last changes fastest.
Arguments:
- wavefunction: bfloat16 [384, 16, 128, 128], P('blk'), may hold values from -6 to 6
- left_env: bfloat16 [16, 384, 128, 128], P('op', 'blk'), may hold values from -0.5 to 0.5
- right_env: bfloat16 [16, 384, 128, 128], P('op', 'blk'), may hold values from -0.125 to 0.125
- left_dims: int32 [384], replicated, may hold values from 32 to 128, as said below
- right_dims: int32 [384], replicated, may hold values from 32 to 128, as said below
- partner: int32 [384, 16], replicated, may hold values from 0 to 383, as said below
Outputs:
- hpsi: bfloat16 [384, 16, 128, 128], P('blk', None, 'op')
Inputs may be any that keep to these rules, and one draw needn't show every extreme that they name: `left_dims`: true dimension of a left block; some block has the full 128. `right_dims`: true dimension of a right block; some block has the full 128. `partner`: right block j lies on index j // 6 of blk; the 16 partners of one left block are distinct; the tiles of the left blocks of one index of blk have at most 2 partners on any one index of blk, and exactly 2 on some index, and some index of blk holds 2 partners of the tiles of every index.
All inputs are finite; a program needn't handle non-finite values.
Results may differ from a plain program's by a relative error of at most 0.005.
Values may be sent and summed in bfloat16 or wider, within the bound.
No kernel may reach another device: no remote copies, remote signals or barrier semaphores. Data moves between devices by JAX's collectives and lax.ppermute only.
A program may use at most 128 MiB of HBM per device.

v0:
```python
import jax
import jax.numpy as jnp
from jax import lax
from jax.sharding import PartitionSpec as P


def route_tables(partner, sectors, pair_count, blocks, capacity):
    device_index = lax.axis_index("blk")
    tile_count = sectors * pair_count
    own_partner = lax.dynamic_slice_in_dim(partner, device_index * sectors, sectors, 0).reshape(
        tile_count
    )
    tile_owner = own_partner // sectors
    order_ids = jnp.arange(tile_count, dtype=jnp.int32)
    earlier = order_ids[None, :] < order_ids[:, None]
    same_owner = tile_owner[None, :] == tile_owner[:, None]
    tile_rank = jnp.sum((earlier & same_owner).astype(jnp.int32), axis=1)
    positions = tile_owner * capacity + tile_rank
    every_owner = (partner // sectors).reshape(blocks, tile_count)
    to_here = (every_owner == device_index).astype(jnp.int32)
    before = jnp.cumsum(to_here, axis=1) - to_here
    slot_ids = jnp.arange(capacity, dtype=jnp.int32)
    slot_hit = to_here[:, :, None] * (before[:, :, None] == slot_ids[None, None, :]).astype(
        jnp.int32
    )
    local_right = (partner % sectors).reshape(blocks, tile_count)
    slot_right = jnp.sum(slot_hit * local_right[:, :, None], axis=1).reshape(blocks * capacity)
    block_ids = jnp.arange(blocks, dtype=jnp.int32)
    left_global = block_ids[:, None] * sectors + (order_ids // pair_count)[None, :]
    slot_left = jnp.sum(slot_hit * left_global[:, :, None], axis=1).reshape(blocks * capacity)
    return (positions, slot_right, slot_left)


def on_device(wavefunction, left_env, right_env, left_dims, right_dims, partner):
    sectors = wavefunction.shape[0]
    pair_count = wavefunction.shape[1]
    tile_rows = wavefunction.shape[2]
    blocks = lax.axis_size("blk")
    quarter = tile_rows // lax.axis_size("op")
    capacity = max(2, 3 * sectors * pair_count // (2 * blocks))
    slot_total = blocks * capacity
    tile_count = sectors * pair_count
    positions, slot_right, slot_left = route_tables(partner, sectors, pair_count, blocks, capacity)
    row_ids = jnp.arange(tile_rows, dtype=jnp.int32)
    own_rows = lax.dynamic_slice_in_dim(left_dims, lax.axis_index("blk") * sectors, sectors)
    own_partner = lax.dynamic_slice_in_dim(partner, lax.axis_index("blk") * sectors, sectors, 0)
    partner_dims = jnp.take(right_dims, own_partner, axis=0)
    row_mask = (row_ids[None, :] < own_rows[:, None]).astype(jnp.bfloat16)
    column_mask = (row_ids[None, None, :] < partner_dims[:, :, None]).astype(jnp.bfloat16)
    masked = wavefunction * row_mask[:, None, :, None] * column_mask[:, :, None, :]

    def add_term(term_index, running):
        left_term = lax.dynamic_index_in_dim(left_env, term_index, 0, keepdims=False)
        product = jnp.einsum(
            "sab,spbc->spac", left_term, masked, preferred_element_type=jnp.float32
        )
        product = product.astype(jnp.bfloat16).reshape(tile_count, tile_rows, tile_rows)
        outgoing = (
            jnp.zeros((slot_total, tile_rows, tile_rows), jnp.bfloat16).at[positions].set(product)
        )
        incoming = lax.all_to_all(
            outgoing.reshape(blocks, capacity, tile_rows, tile_rows),
            "blk",
            split_axis=0,
            concat_axis=0,
            tiled=True,
        )
        incoming = incoming.reshape(slot_total, tile_rows, tile_rows)
        right_term = lax.dynamic_index_in_dim(right_env, term_index, 0, keepdims=False)
        picked = jnp.take(right_term, slot_right, axis=0)
        return running + jnp.einsum(
            "nab,ncb->nac", incoming, picked, preferred_element_type=jnp.float32
        )

    initial = jnp.zeros((slot_total, tile_rows, tile_rows), jnp.float32)
    summed = lax.fori_loop(0, left_env.shape[0], add_term, initial)
    shares = lax.psum_scatter(
        summed.reshape(blocks, capacity, tile_rows, tile_rows),
        "op",
        scatter_dimension=2,
        tiled=True,
    )
    results = shares.astype(jnp.bfloat16)
    returned = lax.all_to_all(results, "blk", split_axis=0, concat_axis=0, tiled=True).reshape(
        slot_total, quarter, tile_rows
    )
    own_tiles = jnp.take(returned, positions, axis=0).reshape(
        sectors, pair_count, quarter, tile_rows
    )
    kept_rows = lax.dynamic_slice_in_dim(row_ids, lax.axis_index("op") * quarter, quarter)
    final_rows = (kept_rows[None, :] < own_rows[:, None]).astype(jnp.bfloat16)
    return own_tiles * final_rows[:, None, :, None] * column_mask[:, :, None, :]


def solution(mesh):
    placed = (
        P("blk", None, None, None),
        P("op", "blk", None, None),
        P("op", "blk", None, None),
        P(),
        P(),
        P(),
    )
    return jax.shard_map(
        on_device, mesh=mesh, in_specs=placed, out_specs=P("blk", None, "op", None), check_vma=False
    )
```

profile of v0, /device:TPU:1, one launch (start us, length us, event | category | flops | bytes accessed | tf_op | source)
XLA Modules:
  0.0 681.1 jit_solution(16663429417300876495)
XLA Ops:
  6.5 0.9 constant_dynamic-slice_fusion
  7.5 0.1 copy.17
  7.6 0.8 fusion.16
  8.4 0.8 add_select_fusion
  9.1 0.8 dynamic_slice.26
  10.0 0.1 and.65
  10.1 0.1 reshape.286
  10.1 1.3 gather_fusion.1
  11.4 0.1 reshape.285
  11.5 0.1 div.36
  11.6 0.2 convert_reduce_fusion
  11.8 0.1 fusion.13
  11.9 0.1 copy.14
  12.0 0.1 mul.93
  12.1 0.1 copy.13
  12.3 0.1 reshape.275
  12.4 0.3 reduce_window_sum.11
  12.7 0.1 multiply_reduce_fusion
  12.8 0.1 copy.15
  12.9 0.1 reshape.272
  13.0 2.0 multiply_multiply_fusion
  15.0 535.5 %while.14 = (s32[]{:T(128)}, f32[128,128,128]{2,1,0:T(8,128)}, s32[96]{0:T(128)S(1)}, bf16[4,6,128,128]{3,2,1,0:T(8,128)(2,1)}, bf16[6,16,128,128]{3,2,1,0:T(8,1...) while((s32[]{:T(128)}, f32[128,128,128]{2,1,0:T(8,128)}, ...), condition=%wide.region_5.6_spmd.clone, body=%wide.region_3.5_spmd.clone.sunk | while | flops 947390848 | bytes 66658336 | solution.py:76
  15.0 3.0 convolution_convert_fusion.2
  18.0 3.0 broadcast.309
  21.0 12.7 %scatter_fusion = bf16[128,128,128]{2,1,0:T(8,128)(2,1)} fusion(bf16[128,128,128]{2,1,0:T(8,128)(2,1)} %broadcast.309, s32[96]{0:T(128)S(1)} %fusion.36, bf16[96,128,128]{2,1,0:T(8,128)(2,1)S(1)} %bitcast.56), kind=kCustom, calls=%fused_computation.3.clone.clone.1 | custom fusion | bytes 9437568 | tf_op jit(solution)/shard_map/while/body/eval_jaxpr/scatter | solution.py:59
  33.7 13.2 %all-to-all-start = ((bf16[64,2,128,128]{3,2,1,0:T(8,128)(2,1)}), bf16[64,2,128,128]{3,2,1,0:T(8,128)(2,1)}, u32[]{:S(2)}, u32[]{:S(2)}) async-start(bf16[64,2,128,128]{3,2,1,0:T(8,128)(2,1)} %bitcast.55), calls=%async_computation | async-start | bytes 8388608 | tf_op jit(solution)/shard_map/while/body/eval_jaxpr/all_to_all | solution.py:61
  46.9 0.9 dynamic-slice_bitcast_fusion.2
  47.8 3.0 gather_fusion
  50.9 91.9 %all-to-all-done = bf16[64,2,128,128]{3,2,1,0:T(8,128)(2,1)} async-done(((bf16[64,2,128,128]{3,2,1,0:T(8,128)(2,1)}), bf16[64,2,128,128]{3,2,1,0:T(8,128)(2,1)}, u32[]{:S(2)}, u32[]{:S(2)}) %all-to-all-start) | async-done | bytes 4194336 | tf_op jit(solution)/shard_map/while/body/eval_jaxpr/all_to_all | solution.py:61
  142.8 9.8 %select_add_fusion.2 = f32[128,128,128]{2,1,0:T(8,128)} fusion(f32[128,128,128]{2,1,0:T(8,128)} %get-tuple-element.224, pred[]{:T(512)S(6)} %compare.3, bf16[128,128,128]{2,1,0:T(8,128)(2,1)} %bitcast.53, bf16[128,128,128]{2,1,0:T(8,128)(2,1)} %gather_fusion, pred[128]{0:T(512)(128)(4,1)S(1)} %compare_and_fusion.3), kind=kOutput, calls=%fused_computation.4.clone.1 | convolution fusion | flops 543162368 | bytes 25165952 | tf_op jit(solution)/shard_map/while/body/eval_jaxpr/nab,ncb->nac/dot_general | solution.py:71
  152.6 3.0 convolution_convert_fusion.2
  155.5 3.0 broadcast.309
  158.5 12.7 %scatter_fusion = bf16[128,128,128]{2,1,0:T(8,128)(2,1)} fusion(bf16[128,128,128]{2,1,0:T(8,128)(2,1)} %broadcast.309, s32[96]{0:T(128)S(1)} %fusion.36, bf16[96,128,128]{2,1,0:T(8,128)(2,1)S(1)} %bitcast.56), kind=kCustom, calls=%fused_computation.3.clone.clone.1 | custom fusion | bytes 9437568 | tf_op jit(solution)/shard_map/while/body/eval_jaxpr/scatter | solution.py:59
  171.2 6.0 all-to-all-start
  177.2 0.9 dynamic-slice_bitcast_fusion.2
  178.1 3.0 gather_fusion
  181.2 91.9 %all-to-all-done = bf16[64,2,128,128]{3,2,1,0:T(8,128)(2,1)} async-done(((bf16[64,2,128,128]{3,2,1,0:T(8,128)(2,1)}), bf16[64,2,128,128]{3,2,1,0:T(8,128)(2,1)}, u32[]{:S(2)}, u32[]{:S(2)}) %all-to-all-start) | async-done | bytes 4194336 | tf_op jit(solution)/shard_map/while/body/eval_jaxpr/all_to_all | solution.py:61
  273.0 12.2 %select_add_fusion.2 = f32[128,128,128]{2,1,0:T(8,128)} fusion(f32[128,128,128]{2,1,0:T(8,128)} %get-tuple-element.224, pred[]{:T(512)S(6)} %compare.3, bf16[128,128,128]{2,1,0:T(8,128)(2,1)} %bitcast.53, bf16[128,128,128]{2,1,0:T(8,128)(2,1)} %gather_fusion, pred[128]{0:T(512)(128)(4,1)S(1)} %compare_and_fusion.3), kind=kOutput, calls=%fused_computation.4.clone.1 | convolution fusion | flops 543162368 | bytes 25165952 | tf_op jit(solution)/shard_map/while/body/eval_jaxpr/nab,ncb->nac/dot_general | solution.py:71
  285.2 3.0 convolution_convert_fusion.2
  288.2 3.0 broadcast.309
  291.1 12.7 %scatter_fusion = bf16[128,128,128]{2,1,0:T(8,128)(2,1)} fusion(bf16[128,128,128]{2,1,0:T(8,128)(2,1)} %broadcast.309, s32[96]{0:T(128)S(1)} %fusion.36, bf16[96,128,128]{2,1,0:T(8,128)(2,1)S(1)} %bitcast.56), kind=kCustom, calls=%fused_computation.3.clone.clone.1 | custom fusion | bytes 9437568 | tf_op jit(solution)/shard_map/while/body/eval_jaxpr/scatter | solution.py:59
  303.8 6.0 all-to-all-start
  309.8 0.9 dynamic-slice_bitcast_fusion.2
  310.8 3.0 gather_fusion
  313.8 91.9 %all-to-all-done = bf16[64,2,128,128]{3,2,1,0:T(8,128)(2,1)} async-done(((bf16[64,2,128,128]{3,2,1,0:T(8,128)(2,1)}), bf16[64,2,128,128]{3,2,1,0:T(8,128)(2,1)}, u32[]{:S(2)}, u32[]{:S(2)}) %all-to-all-start) | async-done | bytes 4194336 | tf_op jit(solution)/shard_map/while/body/eval_jaxpr/all_to_all | solution.py:61
  405.7 12.2 %select_add_fusion.2 = f32[128,128,128]{2,1,0:T(8,128)} fusion(f32[128,128,128]{2,1,0:T(8,128)} %get-tuple-element.224, pred[]{:T(512)S(6)} %compare.3, bf16[128,128,128]{2,1,0:T(8,128)(2,1)} %bitcast.53, bf16[128,128,128]{2,1,0:T(8,128)(2,1)} %gather_fusion, pred[128]{0:T(512)(128)(4,1)S(1)} %compare_and_fusion.3), kind=kOutput, calls=%fused_computation.4.clone.1 | convolution fusion | flops 543162368 | bytes 25165952 | tf_op jit(solution)/shard_map/while/body/eval_jaxpr/nab,ncb->nac/dot_general | solution.py:71
  417.9 3.0 convolution_convert_fusion.2
  420.8 3.0 broadcast.309
  423.8 12.7 %scatter_fusion = bf16[128,128,128]{2,1,0:T(8,128)(2,1)} fusion(bf16[128,128,128]{2,1,0:T(8,128)(2,1)} %broadcast.309, s32[96]{0:T(128)S(1)} %fusion.36, bf16[96,128,128]{2,1,0:T(8,128)(2,1)S(1)} %bitcast.56), kind=kCustom, calls=%fused_computation.3.clone.clone.1 | custom fusion | bytes 9437568 | tf_op jit(solution)/shard_map/while/body/eval_jaxpr/scatter | solution.py:59
  436.5 6.0 all-to-all-start
  442.5 0.9 dynamic-slice_bitcast_fusion.2
  443.4 3.0 gather_fusion
  446.5 91.9 %all-to-all-done = bf16[64,2,128,128]{3,2,1,0:T(8,128)(2,1)} async-done(((bf16[64,2,128,128]{3,2,1,0:T(8,128)(2,1)}), bf16[64,2,128,128]{3,2,1,0:T(8,128)(2,1)}, u32[]{:S(2)}, u32[]{:S(2)}) %all-to-all-start) | async-done | bytes 4194336 | tf_op jit(solution)/shard_map/while/body/eval_jaxpr/all_to_all | solution.py:61
  538.3 12.2 %select_add_fusion.2 = f32[128,128,128]{2,1,0:T(8,128)} fusion(f32[128,128,128]{2,1,0:T(8,128)} %get-tuple-element.224, pred[]{:T(512)S(6)} %compare.3, bf16[128,128,128]{2,1,0:T(8,128)(2,1)} %bitcast.53, bf16[128,128,128]{2,1,0:T(8,128)(2,1)} %gather_fusion, pred[128]{0:T(512)(128)(4,1)S(1)} %compare_and_fusion.3), kind=kOutput, calls=%fused_computation.4.clone.1 | convolution fusion | flops 543162368 | bytes 25165952 | tf_op jit(solution)/shard_map/while/body/eval_jaxpr/nab,ncb->nac/dot_general | solution.py:71
  550.5 79.9 %reduce-scatter.2.cloned.1.call-done = f32[64,2,32,128]{3,2,1,0:T(8,128)} async-done(((f32[64,2,128,128]{3,2,1,0:T(8,128)}), f32[64,2,32,128]{3,2,1,0:T(8,128)}) %reduce-scatter.2.cloned.1.call-update) | async-done | bytes 2097168 | tf_op jit(solution)/shard_map/reduce_scatter | solution.py:77
  630.4 2.9 convert_element_type.60
  633.3 10.6 %all-to-all-start.1 = ((bf16[64,2,32,128]{3,2,1,0:T(8,128)(2,1)}), bf16[64,2,32,128]{3,2,1,0:T(8,128)(2,1)S(1)}, u32[]{:S(2)}, u32[]{:S(2)}) async-start(bf16[64,2,32,128]{3,2,1,0:T(8,128)(2,1)} %convert_element_type.60), calls=%async_computation.2 | async-start | bytes 2097152 | tf_op jit(solution)/shard_map/all_to_all | solution.py:84
  643.9 0.1 and.71
  644.0 0.1 div.38
  644.1 0.1 reduce_sum.23
  644.1 0.1 dynamic_slice.27
  644.3 28.1 %all-to-all-done.1 = bf16[64,2,32,128]{3,2,1,0:T(8,128)(2,1)S(1)} async-done(((bf16[64,2,32,128]{3,2,1,0:T(8,128)(2,1)}), bf16[64,2,32,128]{3,2,1,0:T(8,128)(2,1)S(1)}, u32[]{:S(2)}, u32[]{:S(2)}) %all-to-all-start.1) | async-done | bytes 1048608 | tf_op jit(solution)/shard_map/all_to_all | solution.py:84
  672.4 0.7 gather_fusion.2
  673.2 1.1 multiply_multiply_fusion.1
  (36 shorter events, 0.4 us)
Async XLA Ops:
  6.5 3.6 copy-start
  6.5 6.5 copy-start.1
  6.5 623.9 %reduce-scatter.2.cloned.1.call-start = ((), (), s32[]{:S(2)}) async-start(), calls=%async_computation.3 | async-start | bytes 10485760 | tf_op jit(solution)/shard_map/reduce_scatter | solution.py:77
  33.7 109.1 %all-to-all-start = ((bf16[64,2,128,128]{3,2,1,0:T(8,128)(2,1)}), bf16[64,2,128,128]{3,2,1,0:T(8,128)(2,1)}, u32[]{:S(2)}, u32[]{:S(2)}) async-start(bf16[64,2,128,128]{3,2,1,0:T(8,128)(2,1)} %bitcast.55), calls=%async_computation | async-start | bytes 8388608 | tf_op jit(solution)/shard_map/while/body/eval_jaxpr/all_to_all | solution.py:61
  171.2 101.9 %all-to-all-start = ((bf16[64,2,128,128]{3,2,1,0:T(8,128)(2,1)}), bf16[64,2,128,128]{3,2,1,0:T(8,128)(2,1)}, u32[]{:S(2)}, u32[]{:S(2)}) async-start(bf16[64,2,128,128]{3,2,1,0:T(8,128)(2,1)} %bitcast.55), calls=%async_computation | async-start | bytes 8388608 | tf_op jit(solution)/shard_map/while/body/eval_jaxpr/all_to_all | solution.py:61
  303.8 101.8 %all-to-all-start = ((bf16[64,2,128,128]{3,2,1,0:T(8,128)(2,1)}), bf16[64,2,128,128]{3,2,1,0:T(8,128)(2,1)}, u32[]{:S(2)}, u32[]{:S(2)}) async-start(bf16[64,2,128,128]{3,2,1,0:T(8,128)(2,1)} %bitcast.55), calls=%async_computation | async-start | bytes 8388608 | tf_op jit(solution)/shard_map/while/body/eval_jaxpr/all_to_all | solution.py:61
  436.5 101.9 %all-to-all-start = ((bf16[64,2,128,128]{3,2,1,0:T(8,128)(2,1)}), bf16[64,2,128,128]{3,2,1,0:T(8,128)(2,1)}, u32[]{:S(2)}, u32[]{:S(2)}) async-start(bf16[64,2,128,128]{3,2,1,0:T(8,128)(2,1)} %bitcast.55), calls=%async_computation | async-start | bytes 8388608 | tf_op jit(solution)/shard_map/while/body/eval_jaxpr/all_to_all | solution.py:61
  633.3 39.2 %all-to-all-start.1 = ((bf16[64,2,32,128]{3,2,1,0:T(8,128)(2,1)}), bf16[64,2,32,128]{3,2,1,0:T(8,128)(2,1)S(1)}, u32[]{:S(2)}, u32[]{:S(2)}) async-start(bf16[64,2,32,128]{3,2,1,0:T(8,128)(2,1)} %convert_element_type.60), calls=%async_computation.2 | async-start | bytes 2097152 | tf_op jit(solution)/shard_map/all_to_all | solution.py:84
Sparse Core Ops, SparseCore 0:
  550.6 79.7 reduce-scatter.1
where the time goes:
time: 684 us; the launch traced here: 681 us
  waiting for transfers between devices  475 us (69%)
  local copies, waits for them, and re-layouts  83.6 us (12%)
  matrix products  58.2 us (9%)
  starting transfers between devices  41.7 us (6%)
  between operations  13.5 us (2%)
  other arithmetic  8.45 us (1%)
    all_to_all x4, waiting for transfers between devices, add_term(): lax.all_to_all(outgoing.reshape(blocks, capacity, tile_rows, tile_rows),...  367 us
    reduce_scatter x1, waiting for transfers between devices, on_device(): lax.psum_scatter(summed.reshape(blocks, capacity, tile_rows, tile_rows),...  79.9 us
    scatter x4, local copies, waits for them, and re-layouts, add_term(): jnp.zeros((slot_total, tile_rows, tile_rows), jnp.bfloat16).at[positions]  50.6 us
    dot_general x4, matrix products, add_term(): jnp.einsum('nab,ncb->nac', incoming, picked, preferred_element_type=jnp.f...  46.4 us
    all_to_all x4, starting transfers between devices, add_term(): lax.all_to_all(outgoing.reshape(blocks, capacity, tile_rows, tile_rows),...  31.1 us
    all_to_all x1, waiting for transfers between devices, on_device(): lax.all_to_all(results, 'blk', split_axis=0, concat_axis=0, tiled=True)  28.1 us
  transfers between devices with their start and end apart: 6, of which 6 were waited for; matrix products, arithmetic and copies ran while one was open for 2% of the time, Pallas kernels for 0%

commit v1 on v0

v1 whole, which is shorter than its diff:
```python
import functools

import jax
import jax.numpy as jnp
from jax import lax
from jax.experimental import pallas as pl
from jax.experimental.pallas import tpu as pltpu
from jax.sharding import Mesh
from jax.sharding import PartitionSpec as P

STEPS = (0, 1, -1, 2, -2, 3, -3, 4)
CHUNKS = ((0, 3), (3, 5), (5, 8))
CAP = 2


def shift(array, axis, by):
    count = lax.axis_size(axis)
    return lax.ppermute(array, axis, [(i, (i + by) % count) for i in range(count)])


def both_ways(array, axis):
    half = array.shape[0] // 2
    before, after = shift(array, axis, 1), shift(array, axis, -1)
    far = jnp.concatenate([shift(before[:half], axis, 1), shift(after[half:], axis, -1)], 0)
    return before, after, far


def ring_of_eight(array, axis):
    half = array.shape[0] // 2
    before = after = array
    held = [array]
    for _ in range(3):
        before, after = shift(before, axis, 1), shift(after, axis, -1)
        held += [after, before]
    held.append(jnp.concatenate([shift(before[:half], axis, 1), shift(after[half:], axis, -1)], 0))
    return held


def first_and_last(hit, keys, top):
    return jnp.stack(
        [jnp.min(jnp.where(hit, keys, top), -1), jnp.max(jnp.where(hit, keys, 0), -1)], -1
    )


def chunk_kernel(first, count, where, left_at, right_at, *refs):
    left, pieces, rights, out, tile = refs[0], refs[1:5], refs[5 : 5 + count], refs[-2], refs[-1]
    here = where[0]
    sources, terms = left.shape[0], left.shape[2]
    rows = pieces[0].shape[-2]
    size = left.shape[-1]

    def one_source(source, _):
        for step in range(count):
            for rank in range(CAP):
                slot = (source * len(STEPS) + first + step) * CAP + rank
                i, j = left_at[slot], right_at[slot]
                for away, piece in enumerate(pieces):
                    quarter = lax.rem(here + (0, 3, 1, 2)[away], 4)
                    tile[step * CAP + rank, pl.ds(pl.multiple_of(quarter * rows, rows), rows)] = (
                        piece[source, first + step, rank]
                    )
                psi = tile[step * CAP + rank]
                total = jnp.zeros((size, size), jnp.float32)
                for term in range(terms):
                    product = jnp.dot(
                        left[source, i, term], psi, preferred_element_type=jnp.float32
                    ).astype(jnp.bfloat16)
                    total += lax.dot_general(
                        product,
                        rights[step][j, term],
                        (((1,), (1,)), ((), ())),
                        preferred_element_type=jnp.float32,
                    )
                total = total.astype(jnp.bfloat16)
                for quarter in range(4):
                    out[quarter, source, step, rank] = total[quarter * rows : (quarter + 1) * rows]
        return 0

    lax.fori_loop(0, sources, one_source, 0)


def compute_chunk(first, count, where, left_at, right_at, left, pieces, rights):
    sources, _, terms, size, _ = left.shape
    rows = pieces[0].shape[-2]
    slots = sources * count * CAP
    smem = pl.BlockSpec(memory_space=pltpu.SMEM)
    vmem = pl.BlockSpec(memory_space=pltpu.VMEM)
    return pl.pallas_call(
        functools.partial(chunk_kernel, first, count),
        out_shape=jax.ShapeDtypeStruct((4, sources, count, CAP, rows, size), jnp.bfloat16),
        in_specs=[smem] * 3 + [vmem] * (5 + count),
        out_specs=vmem,
        scratch_shapes=[pltpu.VMEM((count * CAP, size, size), jnp.bfloat16)],
        compiler_params=pltpu.CompilerParams(vmem_limit_bytes=50 * 1024 * 1024),
        cost_estimate=pl.CostEstimate(
            flops=slots * terms * 4 * size**3 * 4,
            bytes_accessed=slots * size * size * 4,
            transcendentals=0,
        ),
    )(where, left_at, right_at, left, *pieces, *rights)


def on_device(wavefunction, left_env, right_env, left_dims, right_dims, partner):
    sectors, pairs, size, _ = wavefunction.shape
    tiles = sectors * pairs
    x, z, k, y = (lax.axis_index(name) for name in ("x", "z", "k", "y"))
    nx, nz, nk, ny = (lax.axis_size(name) for name in ("x", "z", "k", "y"))
    rows = size // ny
    steps = jnp.array(STEPS, jnp.int32)
    place = jnp.array([STEPS.index(d if d <= 4 else d - nz) for d in range(nz)], jnp.int32)

    left_all = lax.all_gather(jnp.swapaxes(left_env, 0, 1), ("x", "k"))
    rights = ring_of_eight(jnp.swapaxes(right_env, 0, 1), "z")

    block = (x * nz + z) * nk + k
    own_partner = lax.dynamic_slice_in_dim(partner, block * sectors, sectors, 0).reshape(tiles)
    own_dims = lax.dynamic_slice_in_dim(left_dims, block * sectors, sectors, 0)
    owner = own_partner // sectors
    order = jnp.arange(tiles, dtype=jnp.int32)
    zs = (z + steps) % nz
    xs, ks = jnp.arange(nx, dtype=jnp.int32), jnp.arange(nk, dtype=jnp.int32)
    targets = ((xs[:, None, None] * nz + zs) * nk + ks[:, None]).reshape(nx * nk * nz)
    sent = first_and_last(targets[:, None] == owner, order, tiles - 1).reshape(-1)
    columns = jnp.arange(size, dtype=jnp.int32)
    own_rows = lax.dynamic_slice_in_dim(columns, y * rows, rows)
    row_mask = (own_rows < jnp.repeat(own_dims, pairs)[:, None]).astype(jnp.bfloat16)
    column_mask = (columns < jnp.take(right_dims, own_partner)[:, None]).astype(jnp.bfloat16)
    mask = row_mask[:, :, None] * column_mask[:, None, :]
    quarter = lax.dynamic_slice_in_dim(wavefunction, y * rows, rows, 2).reshape(tiles, rows, size)
    outgoing = jnp.take(quarter * mask, sent, axis=0, mode="clip")
    incoming = lax.all_to_all(
        outgoing.reshape(nx * nk, nz, CAP, rows, size), ("x", "k"), 0, 0, tiled=True
    )
    pieces = (incoming, *both_ways(incoming, "y"))

    group = lax.dynamic_index_in_dim(partner.reshape(nx, nz, nk, tiles), z, 1, keepdims=False)
    group = group.reshape(nx * nk, 1, tiles)
    wanted = ((x * nz + zs) * nk + k)[None, :, None]
    keys = first_and_last(
        group // sectors == wanted, order * 8 + group % sectors, (tiles - 1) * 8 + sectors - 1
    ).reshape(-1)
    left_at, right_at = keys // (8 * pairs), jnp.minimum(keys % 8, sectors - 1)

    where = y.astype(jnp.int32).reshape(1)
    parts = []
    for first, last in CHUNKS:
        partial = compute_chunk(
            first, last - first, where, left_at, right_at, left_all, pieces, rights[first:last]
        )
        shares = lax.all_to_all(partial, "y", 0, 0, tiled=True)
        parts.append(jnp.sum(shares.astype(jnp.float32), 0).astype(jnp.bfloat16))
    finished = jnp.concatenate(parts, 1)
    returned = lax.all_to_all(finished, ("x", "k"), 0, 0, tiled=True)
    returned = returned.reshape(nx * nk * nz * CAP, rows, size)

    lane = owner // (nz * nk) * nk + owner % nk
    again = jnp.any((owner[None, :] == owner[:, None]) & (order[None, :] < order[:, None]), 1)
    spot = (lane * nz + jnp.take(place, (owner // nk - z) % nz)) * CAP + again.astype(jnp.int32)
    own = jnp.take(returned, spot, axis=0, mode="clip") * mask
    return own.reshape(sectors, pairs, rows, size)


def solution(mesh):
    fine = Mesh(mesh.devices.reshape(4, 8, 2, 4), ("x", "z", "k", "y"))
    blk = ("x", "z", "k")
    placed = (P(blk), P("y", blk), P("y", blk), P(), P(), P())
    return jax.shard_map(
        on_device, mesh=fine, in_specs=placed, out_specs=P(blk, None, "y", None), check_vma=False
    )
```

time: 684 us -> 236 us (0.35)
  waiting for transfers between devices: 475 us -> 55.1 us
  matrix products: 58.2 us -> 0 us
  local copies, waits for them, and re-layouts: 83.6 us -> 31 us
  Pallas kernels: 0 us -> 44.5 us
  blocking collectives: 0 us -> 32.3 us
    all_to_all x5 -> x4, waiting for transfers between devices: 396 us -> 25.2 us  [the longest x1 14.3 us: on_device(): returned = lax.all_to_all(finished, ('x', 'k'), 0, 0, tiled=True)]
    reduce_scatter x1 -> x0, waiting for transfers between devices: 79.9 us -> none  [on_device(): lax.psum_scatter(summed.reshape(blocks, capacity, tile_rows, tile_rows),...]
    dot_general x8 -> x0, matrix products: 58.2 us -> none  [the longest x4 46.4 us: add_term(): jnp.einsum('nab,ncb->nac', incoming, picked, preferred_element_type=jnp.f...]
    scatter x4 -> x0, local copies, waits for them, and re-layouts: 50.6 us -> none  [add_term(): jnp.zeros((slot_total, tile_rows, tile_rows), jnp.bfloat16).at[positions]]
    pallas_call x0 -> x3, Pallas kernels: none -> 44.5 us  [compute_chunk(): pl.pallas_call(functools.partial(chunk_kernel, first, count), out_shape=j...]
    all_to_all x0 -> x1, blocking collectives: none -> 32.3 us  [on_device(): lax.all_to_all(outgoing.reshape(nx * nk, nz, CAP, rows, size), ('x', 'k')...]
    ppermute x0 -> x12, waiting for transfers between devices: none -> 29.2 us  [shift(): lax.ppermute(array, axis, [(i, (i + by) % count) for i in range(count)])]
    ppermute x0 -> x12, starting transfers between devices: none -> 19.5 us  [shift(): lax.ppermute(array, axis, [(i, (i + by) % count) for i in range(count)])]
  transfers between devices with their start and end apart: 6 -> 17, of which waited for: 6 -> 6; matrix products, arithmetic and copies ran while one was open for 2% -> 15% of each run, Pallas kernels for 0% -> 14%
where the time goes in v1:
time: 236 us; the launch traced here: 235 us
  waiting for transfers between devices  55.1 us (23%)
  Pallas kernels  44.5 us (19%)
  starting transfers between devices  43.4 us (18%)
  blocking collectives  32.3 us (14%)
  local copies, waits for them, and re-layouts  31 us (13%)
  other arithmetic  15.2 us (6%)
  between operations  13.7 us (6%)
    pallas_call x3, Pallas kernels, compute_chunk(): pl.pallas_call(functools.partial(chunk_kernel, first, count), out_shape=j...  44.5 us
    all_to_all x1, blocking collectives, on_device(): lax.all_to_all(outgoing.reshape(nx * nk, nz, CAP, rows, size), ('x', 'k')...  32.3 us
    ppermute x12, waiting for transfers between devices, shift(): lax.ppermute(array, axis, [(i, (i + by) % count) for i in range(count)])  29.2 us
    ppermute x12, starting transfers between devices, shift(): lax.ppermute(array, axis, [(i, (i + by) % count) for i in range(count)])  19.5 us
    all_to_all x1, waiting for transfers between devices, on_device(): returned = lax.all_to_all(finished, ('x', 'k'), 0, 0, tiled=True)  14.3 us
    all_to_all x3, starting transfers between devices, on_device(): shares = lax.all_to_all(partial, 'y', 0, 0, tiled=True)  12.9 us
    all_to_all x1, starting transfers between devices, on_device(): returned = lax.all_to_all(finished, ('x', 'k'), 0, 0, tiled=True)  11 us
    all_to_all x3, waiting for transfers between devices, on_device(): shares = lax.all_to_all(partial, 'y', 0, 0, tiled=True)  10.9 us
  transfers between devices with their start and end apart: 17, of which 6 were waited for; matrix products, arithmetic and copies ran while one was open for 15% of the time, Pallas kernels for 14%

profile of v1, /device:TPU:1, one launch (start us, length us, event | category | flops | bytes accessed | tf_op | source)
XLA Modules:
  0.0 235.3 jit_solution(8546445408346421666)
XLA Ops:
  6.5 0.7 all-gather.3.cloned.1.call-update
  7.3 1.1 copy.20
  8.4 0.1 reshape.535
  8.5 0.1 reshape.536
  8.5 0.8 dynamic_slice.19
  9.3 0.7 multiply_add_fusion
  10.0 0.1 add.295
  10.2 0.1 lt.158
  10.3 0.2 fusion.6
  10.5 0.1 copy.24
  10.6 0.1 reshape.550
  10.7 0.1 dynamic_slice.18
  10.8 0.2 fusion.2
  11.1 1.6 gather_fusion
  12.7 0.1 constant_dynamic-slice_fusion.1
  12.8 0.1 fusion
  12.9 0.1 compare_convert_fusion.1
  13.0 1.4 bitcast_multiply_fusion
  14.3 2.8 %gather_fusion.1 = bf16[128,32,128]{2,1,0:T(8,128)(2,1)} fusion(bf16[96,32,128]{2,1,0:T(8,128)(2,1)} %bitcast_multiply_fusion, s32[1024]{0:T(1024)S(1)} %get-tuple-element.19), kind=kCustom, calls=%fused_computation.1 | custom fusion | bytes 2097664 | tf_op jit(solution)/shard_map/jit(_take)/gather | solution.py:130
  17.1 32.3 %all_to_all.25.refs_1_ = bf16[8,8,2,32,128]{4,3,2,1,0:T(8,128)(2,1)} all-to-all(bf16[8,8,2,32,128]{4,3,2,1,0:T(8,128)(2,1)} %bitcast.52), channel_id=1, replica_groups=mesh['x'=4,'z'=8,'k'=2,'y'=4] {'x','k'}, dimensions={0} | all-to-all | bytes 2097152 | tf_op jit(solution)/shard_map/all_to_all | solution.py:131
  49.5 2.7 %collective-permute-start.1 = (bf16[8,8,2,32,128]{4,3,2,1,0:T(8,128)(2,1)}, bf16[8,8,2,32,128]{4,3,2,1,0:T(8,128)(2,1)}, u32[]{:S(2)}, u32[]{:S(2)}) collective-permute-start(bf16[8,8,2,32,128]{4,3,2,1,0:T(8,128)(2,1)} %all_to_all.25.refs_1_), channel_id=1, source_target_pairs={{0,3},{1,0},{2,1},{3,2},{4,7},{5,4},{6,5},{7,6},{8,11},{9,8},{10,9... | collective-permute-start | bytes 3145736 | tf_op jit(solution)/shard_map/ppermute | solution.py:18
  52.1 2.1 copy.27
  54.2 5.9 %collective-permute-start.4 = (bf16[6,4,128,128]{3,2,1,0:T(8,128)(2,1)}, bf16[6,4,128,128]{3,2,1,0:T(8,128)(2,1)}, u32[]{:S(2)}, u32[]{:S(2)}) collective-permute-start(bf16[6,4,128,128]{3,2,1,0:T(8,128)(2,1)} %bitcast.48.refs_5_), channel_id=1, source_target_pairs={{0,56},{8,0},{16,8},{24,16},{32,24},{40,32},{48,40},{56,48},{1,57}... | collective-permute-start | bytes 2359304 | tf_op jit(solution)/shard_map/ppermute | solution.py:18
  60.1 0.1 reshape.532
  60.3 17.0 %collective-permute-done.5.refs_7_ = bf16[6,4,128,128]{3,2,1,0:T(8,128)(2,1)} collective-permute-done((bf16[6,4,128,128]{3,2,1,0:T(8,128)(2,1)}, bf16[6,4,128,128]{3,2,1,0:T(8,128)(2,1)}, u32[]{:S(2)}, u32[]{:S(2)}) %collective-permute-start.5) | collective-permute-done | bytes 786464 | tf_op jit(solution)/shard_map/ppermute | solution.py:18
  77.3 2.7 %collective-permute-start.6 = (bf16[6,4,128,128]{3,2,1,0:T(8,128)(2,1)}, bf16[6,4,128,128]{3,2,1,0:T(8,128)(2,1)}, u32[]{:S(2)}, u32[]{:S(2)}) collective-permute-start(bf16[6,4,128,128]{3,2,1,0:T(8,128)(2,1)} %collective-permute-done.4.refs_6_), channel_id=1, source_target_pairs={{0,56},{8,0},{16,8},{24,16},{32,24},{40,32},{48,40},{56,48},{1,57}... | collective-permute-start | bytes 2359304 | tf_op jit(solution)/shard_map/ppermute | solution.py:18
  80.0 1.9 slice.31
  81.9 1.9 slice.32
  83.8 2.7 %collective-permute-start.3 = (bf16[4,8,2,32,128]{4,3,2,1,0:T(8,128)(2,1)}, bf16[4,8,2,32,128]{4,3,2,1,0:T(8,128)(2,1)}, u32[]{:S(2)}, u32[]{:S(2)}) collective-permute-start(bf16[4,8,2,32,128]{4,3,2,1,0:T(8,128)(2,1)} %slice.32), channel_id=1, source_target_pairs={{0,3},{1,0},{2,1},{3,2},{4,7},{5,4},{6,5},{7,6},{8,11},{9,8},{10,9... | collective-permute-start | bytes 1572872 | tf_op jit(solution)/shard_map/ppermute | solution.py:18
  86.4 0.4 fusion.4
  86.9 0.1 copy.21
  87.0 0.1 reshape.533
  87.1 7.5 %collective-permute-done.2 = bf16[4,8,2,32,128]{4,3,2,1,0:T(8,128)(2,1)} collective-permute-done((bf16[4,8,2,32,128]{4,3,2,1,0:T(8,128)(2,1)}, bf16[4,8,2,32,128]{4,3,2,1,0:T(8,128)(2,1)}, u32[]{:S(2)}, u32[]{:S(2)}) %collective-permute-start.2) | collective-permute-done | bytes 524320 | tf_op jit(solution)/shard_map/ppermute | solution.py:18
  94.6 1.9 constant_dynamic-update-slice_fusion.1
  96.5 1.9 constant_dynamic-update-slice_fusion.refs_4_
  98.4 8.0 %copy.22 = bf16[48,4,128,128]{3,2,1,0:T(8,128)(2,1)} copy(bf16[48,4,128,128]{3,2,0,1:T(8,128)(2,1)} %all-gather.3.cloned.1.call-done) | data formatting | bytes 12582912 | tf_op jit(solution)/shard_map/all_gather | solution.py:112
  106.4 12.0 %shard_map.83 = bf16[4,8,2,2,32,128]{5,4,3,2,1,0:T(8,128)(2,1)S(1)} custom-call(s32[1]{0:T(128)} %bitcast.where, s32[128]{0:T(128)S(1)} %get-tuple-element.18.left_at, s32[128]{0:T(128)S(1)} %get-tuple-element.17.right_at, bf16[8,6,4,128,128]{4,3,2,1,0:T(8,128)(2,1)} %bitcast.49, bf16[8,8,2,32,128]{4,3,2,1,0:T(8,128)(2,1)} %all_to_all.25.refs_1_, ...), custom_call_target="tpu_custom_call" | custom-call | flops 4294967296 | bytes 2097152 | tf_op jit(solution)/shard_map/pallas_call | solution.py:88
  118.5 1.0 copy-done.1
  119.5 4.2 %all-to-all-start.2 = ((bf16[4,8,2,2,32,128]{5,4,3,2,1,0:T(8,128)(2,1)}), bf16[4,8,2,2,32,128]{5,4,3,2,1,0:T(8,128)(2,1)}, u32[]{:S(2)}, u32[]{:S(2)}) async-start(bf16[4,8,2,2,32,128]{5,4,3,2,1,0:T(8,128)(2,1)} %copy-done.1), calls=%async_computation.2 | async-start | bytes 2097152 | tf_op jit(solution)/shard_map/all_to_all | solution.py:150
  123.7 0.1 collective-permute-start.9
  123.8 2.7 %collective-permute-start.8 = (bf16[6,4,128,128]{3,2,1,0:T(8,128)(2,1)}, bf16[6,4,128,128]{3,2,1,0:T(8,128)(2,1)}, u32[]{:S(2)}, u32[]{:S(2)}) collective-permute-start(bf16[6,4,128,128]{3,2,1,0:T(8,128)(2,1)} %collective-permute-done.6.refs_5_), channel_id=1, source_target_pairs={{0,56},{8,0},{16,8},{24,16},{32,24},{40,32},{48,40},{56,48},{1,57}... | collective-permute-start | bytes 2359304 | tf_op jit(solution)/shard_map/ppermute | solution.py:18
  126.5 16.4 %shard_map.82 = bf16[4,8,3,2,32,128]{5,4,3,2,1,0:T(8,128)(2,1)} custom-call(s32[1]{0:T(128)} %bitcast.where, s32[128]{0:T(128)S(1)} %get-tuple-element.18.left_at, s32[128]{0:T(128)S(1)} %get-tuple-element.17.right_at, bf16[8,6,4,128,128]{4,3,2,1,0:T(8,128)(2,1)} %bitcast.50, bf16[8,8,2,32,128]{4,3,2,1,0:T(8,128)(2,1)} %all_to_all.25.refs_1_, ...), custom_call_target="tpu_custom_call" | custom-call | flops 6442450944 | bytes 3145728 | tf_op jit(solution)/shard_map/pallas_call | solution.py:88
  142.9 4.3 %all-to-all-start.1 = ((bf16[4,8,3,2,32,128]{5,4,3,2,1,0:T(8,128)(2,1)}), bf16[4,8,3,2,32,128]{5,4,3,2,1,0:T(8,128)(2,1)}, u32[]{:S(2)}, u32[]{:S(2)}) async-start(bf16[4,8,3,2,32,128]{5,4,3,2,1,0:T(8,128)(2,1)} %shard_map.82), calls=%async_computation.1 | async-start | bytes 3145728 | tf_op jit(solution)/shard_map/all_to_all | solution.py:150
  147.2 1.0 slice.33
  148.3 0.1 collective-permute-start.10
  148.4 1.0 slice.34
  149.4 2.7 %collective-permute-start.11 = (bf16[3,4,128,128]{3,2,1,0:T(8,128)(2,1)S(1)}, bf16[3,4,128,128]{3,2,1,0:T(8,128)(2,1)S(1)}, u32[]{:S(2)}, u32[]{:S(2)}) collective-permute-start(bf16[3,4,128,128]{3,2,1,0:T(8,128)(2,1)S(1)} %slice.34), channel_id=1, source_target_pairs={{0,56},{8,0},{16,8},{24,16},{32,24},{40,32},{48,40},{56,48},{1,57}... | collective-permute-start | bytes 1179656 | tf_op jit(solution)/shard_map/ppermute | solution.py:18
  152.1 4.5 %collective-permute-done.10 = bf16[3,4,128,128]{3,2,1,0:T(8,128)(2,1)S(1)} collective-permute-done((bf16[3,4,128,128]{3,2,1,0:T(8,128)(2,1)S(1)}, bf16[3,4,128,128]{3,2,1,0:T(8,128)(2,1)S(1)}, u32[]{:S(2)}, u32[]{:S(2)}) %collective-permute-start.10) | collective-permute-done | bytes 393248 | tf_op jit(solution)/shard_map/ppermute | solution.py:18
  156.6 0.3 collective-permute-done.11
  156.9 16.1 %shard_map.84 = bf16[4,8,3,2,32,128]{5,4,3,2,1,0:T(8,128)(2,1)} custom-call(s32[1]{0:T(128)} %bitcast.where, s32[128]{0:T(128)S(1)} %get-tuple-element.18.left_at, s32[128]{0:T(128)S(1)} %get-tuple-element.17.right_at, bf16[8,6,4,128,128]{4,3,2,1,0:T(8,128)(2,1)} %bitcast.51, bf16[8,8,2,32,128]{4,3,2,1,0:T(8,128)(2,1)} %all_to_all.25.refs_1_, ...), custom_call_target="tpu_custom_call" | custom-call | flops 6442450944 | bytes 3145728 | tf_op jit(solution)/shard_map/pallas_call | solution.py:88
  173.0 4.4 %all-to-all-start.3 = ((bf16[4,8,3,2,32,128]{5,4,3,2,1,0:T(8,128)(2,1)}), bf16[4,8,3,2,32,128]{5,4,3,2,1,0:T(8,128)(2,1)}, u32[]{:S(2)}, u32[]{:S(2)}) async-start(bf16[4,8,3,2,32,128]{5,4,3,2,1,0:T(8,128)(2,1)} %shard_map.84), calls=%async_computation.3 | async-start | bytes 3145728 | tf_op jit(solution)/shard_map/all_to_all | solution.py:150
  177.4 2.2 reduce_sum.37
  179.6 1.7 reduce_sum.36
  181.3 10.9 %all-to-all-done.3 = bf16[4,8,3,2,32,128]{5,4,3,2,1,0:T(8,128)(2,1)} async-done(((bf16[4,8,3,2,32,128]{5,4,3,2,1,0:T(8,128)(2,1)}), bf16[4,8,3,2,32,128]{5,4,3,2,1,0:T(8,128)(2,1)}, u32[]{:S(2)}, u32[]{:S(2)}) %all-to-all-start.3) | async-done | bytes 1572896 | tf_op jit(solution)/shard_map/all_to_all | solution.py:150
  192.2 2.6 %reduce_sum.38 = bf16[8,3,2,32,128]{4,3,2,1,0:T(8,128)(2,1)} reduce(bf16[4,8,3,2,32,128]{5,4,3,2,1,0:T(8,128)(2,1)} %all-to-all-done.3, bf16[]{:T(256)} %constant.170.clone.1), dimensions={0}, to_apply=%region_6.7 | reduce | flops 589824 | bytes 1966082 | tf_op jit(solution)/shard_map/reduce_sum | solution.py:151
  194.8 2.1 pad_maximum_fusion
  196.9 11.0 %all-to-all-start.4 = ((bf16[8,8,2,32,128]{4,3,2,1,0:T(8,128)(2,1)}), bf16[8,8,2,32,128]{4,3,2,1,0:T(8,128)(2,1)}, u32[]{:S(2)}, u32[]{:S(2)}) async-start(bf16[8,8,2,32,128]{4,3,2,1,0:T(8,128)(2,1)} %pad_maximum_fusion), calls=%async_computation.4 | async-start | bytes 2097152 | tf_op jit(solution)/shard_map/all_to_all | solution.py:153
  208.0 0.1 gather.28
  208.0 0.7 and_select_fusion
  208.7 0.1 compare_convert_fusion
  208.8 0.1 fusion.3
  208.9 14.3 %all-to-all-done.4 = bf16[8,8,2,32,128]{4,3,2,1,0:T(8,128)(2,1)} async-done(((bf16[8,8,2,32,128]{4,3,2,1,0:T(8,128)(2,1)}), bf16[8,8,2,32,128]{4,3,2,1,0:T(8,128)(2,1)}, u32[]{:S(2)}, u32[]{:S(2)}) %all-to-all-start.4) | async-done | bytes 1048608 | tf_op jit(solution)/shard_map/all_to_all | solution.py:153
  223.2 2.8 %gather_fusion.2 = bf16[96,32,128]{2,1,0:T(8,128)(2,1)} fusion(bf16[128,32,128]{2,1,0:T(8,128)(2,1)} %bitcast.13, s32[1024]{0:T(1024)S(1)} %pad_clamp_fusion), kind=kCustom, calls=%fused_computation.2 | custom fusion | bytes 1573248 | tf_op jit(solution)/shard_map/jit(_take)/gather | solution.py:159
  226.0 2.5 %multiply_multiply_fusion = bf16[6,16,32,128]{3,2,1,0:T(8,128)(2,1)} fusion(bf16[6,16,32,128]{3,2,1,0:T(8,128)(2,1)} %bitcast.53, bf16[6,16,128]{2,1,0:T(8,128)(2,1)S(1)} %fusion.3, bf16[6,16,32]{2,1,0:T(8,128)(2,1)S(1)} %compare_convert_fusion), kind=kLoop, calls=%fused_computation.7 | loop fusion | flops 786432 | bytes 1603584 | tf_op jit(solution)/shard_map/mul | solution.py:159
  (41 shorter events, 0.4 us)
Async XLA Ops:
  6.5 6.2 %copy-start = (bf16[6,16,128,128]{3,2,1,0:T(8,128)(2,1)S(1)}, bf16[6,16,128,128]{3,2,1,0:T(8,128)(2,1)}, u32[]{:S(2)}) copy-start(bf16[6,16,128,128]{3,2,1,0:T(8,128)(2,1)} %param.8) | copy-start | bytes 9437188
  6.5 91.9 %all-gather.3.cloned.1.call-start = ((), (), s32[]{:S(2)}) async-start(), calls=%async_computation.5 | async-start | bytes 7077888 | tf_op jit(solution)/shard_map/all_gather | solution.py:112
  8.3 51.8 %copy-start.2 = (s32[384,16]{1,0:T(8,128)}, s32[384,16]{1,0:T(8,128)S(1)}, u32[]{:S(2)}) copy-start(s32[384,16]{1,0:T(8,128)S(1)} %copy.20) | copy-start | bytes 73732
  49.5 30.5 %collective-permute-start = (bf16[8,8,2,32,128]{4,3,2,1,0:T(8,128)(2,1)}, bf16[8,8,2,32,128]{4,3,2,1,0:T(8,128)(2,1)}, u32[]{:S(2)}, u32[]{:S(2)}) collective-permute-start(bf16[8,8,2,32,128]{4,3,2,1,0:T(8,128)(2,1)} %all_to_all.25.refs_1_), channel_id=1, source_target_pairs={{0,1},{1,2},{2,3},{3,0},{4,5},{5,6},{6,7},{7,4},{8,9},{9,10},{10,1... | collective-permute-start | bytes 3145736 | tf_op jit(solution)/shard_map/ppermute | solution.py:18
  49.5 32.4 %collective-permute-start.1 = (bf16[8,8,2,32,128]{4,3,2,1,0:T(8,128)(2,1)}, bf16[8,8,2,32,128]{4,3,2,1,0:T(8,128)(2,1)}, u32[]{:S(2)}, u32[]{:S(2)}) collective-permute-start(bf16[8,8,2,32,128]{4,3,2,1,0:T(8,128)(2,1)} %all_to_all.25.refs_1_), channel_id=1, source_target_pairs={{0,3},{1,0},{2,1},{3,2},{4,7},{5,4},{6,5},{7,6},{8,11},{9,8},{10,9... | collective-permute-start | bytes 3145736 | tf_op jit(solution)/shard_map/ppermute | solution.py:18
  54.2 23.1 %collective-permute-start.5 = (bf16[6,4,128,128]{3,2,1,0:T(8,128)(2,1)}, bf16[6,4,128,128]{3,2,1,0:T(8,128)(2,1)}, u32[]{:S(2)}, u32[]{:S(2)}) collective-permute-start(bf16[6,4,128,128]{3,2,1,0:T(8,128)(2,1)} %bitcast.48.refs_5_), channel_id=1, source_target_pairs={{0,8},{8,16},{16,24},{24,32},{32,40},{40,48},{48,56},{56,0},{1,9},... | collective-permute-start | bytes 2359304 | tf_op jit(solution)/shard_map/ppermute | solution.py:18
  54.2 23.1 %collective-permute-start.4 = (bf16[6,4,128,128]{3,2,1,0:T(8,128)(2,1)}, bf16[6,4,128,128]{3,2,1,0:T(8,128)(2,1)}, u32[]{:S(2)}, u32[]{:S(2)}) collective-permute-start(bf16[6,4,128,128]{3,2,1,0:T(8,128)(2,1)} %bitcast.48.refs_5_), channel_id=1, source_target_pairs={{0,56},{8,0},{16,8},{24,16},{32,24},{40,32},{48,40},{56,48},{1,57}... | collective-permute-start | bytes 2359304 | tf_op jit(solution)/shard_map/ppermute | solution.py:18
  77.3 29.1 %collective-permute-start.7 = (bf16[6,4,128,128]{3,2,1,0:T(8,128)(2,1)}, bf16[6,4,128,128]{3,2,1,0:T(8,128)(2,1)}, u32[]{:S(2)}, u32[]{:S(2)}) collective-permute-start(bf16[6,4,128,128]{3,2,1,0:T(8,128)(2,1)} %collective-permute-done.5.refs_7_), channel_id=1, source_target_pairs={{0,8},{8,16},{16,24},{24,32},{32,40},{40,48},{48,56},{56,0},{1,9},... | collective-permute-start | bytes 2359304 | tf_op jit(solution)/shard_map/ppermute | solution.py:18
  77.3 29.1 %collective-permute-start.6 = (bf16[6,4,128,128]{3,2,1,0:T(8,128)(2,1)}, bf16[6,4,128,128]{3,2,1,0:T(8,128)(2,1)}, u32[]{:S(2)}, u32[]{:S(2)}) collective-permute-start(bf16[6,4,128,128]{3,2,1,0:T(8,128)(2,1)} %collective-permute-done.4.refs_6_), channel_id=1, source_target_pairs={{0,56},{8,0},{16,8},{24,16},{32,24},{40,32},{48,40},{56,48},{1,57}... | collective-permute-start | bytes 2359304 | tf_op jit(solution)/shard_map/ppermute | solution.py:18
  81.9 12.8 %collective-permute-start.2 = (bf16[4,8,2,32,128]{4,3,2,1,0:T(8,128)(2,1)}, bf16[4,8,2,32,128]{4,3,2,1,0:T(8,128)(2,1)}, u32[]{:S(2)}, u32[]{:S(2)}) collective-permute-start(bf16[4,8,2,32,128]{4,3,2,1,0:T(8,128)(2,1)} %slice.31), channel_id=1, source_target_pairs={{0,1},{1,2},{2,3},{3,0},{4,5},{5,6},{6,7},{7,4},{8,9},{9,10},{10,1... | collective-permute-start | bytes 1572872 | tf_op jit(solution)/shard_map/ppermute | solution.py:18
  83.8 12.7 %collective-permute-start.3 = (bf16[4,8,2,32,128]{4,3,2,1,0:T(8,128)(2,1)}, bf16[4,8,2,32,128]{4,3,2,1,0:T(8,128)(2,1)}, u32[]{:S(2)}, u32[]{:S(2)}) collective-permute-start(bf16[4,8,2,32,128]{4,3,2,1,0:T(8,128)(2,1)} %slice.32), channel_id=1, source_target_pairs={{0,3},{1,0},{2,1},{3,2},{4,7},{5,4},{6,5},{7,6},{8,11},{9,8},{10,9... | collective-permute-start | bytes 1572872 | tf_op jit(solution)/shard_map/ppermute | solution.py:18
  118.4 1.1 copy-start.1
  119.5 23.4 %all-to-all-start.2 = ((bf16[4,8,2,2,32,128]{5,4,3,2,1,0:T(8,128)(2,1)}), bf16[4,8,2,2,32,128]{5,4,3,2,1,0:T(8,128)(2,1)}, u32[]{:S(2)}, u32[]{:S(2)}) async-start(bf16[4,8,2,2,32,128]{5,4,3,2,1,0:T(8,128)(2,1)} %copy-done.1), calls=%async_computation.2 | async-start | bytes 2097152 | tf_op jit(solution)/shard_map/all_to_all | solution.py:150
  123.7 23.5 %collective-permute-start.9 = (bf16[6,4,128,128]{3,2,1,0:T(8,128)(2,1)}, bf16[6,4,128,128]{3,2,1,0:T(8,128)(2,1)}, u32[]{:S(2)}, u32[]{:S(2)}) collective-permute-start(bf16[6,4,128,128]{3,2,1,0:T(8,128)(2,1)} %collective-permute-done.7.refs_6_), channel_id=1, source_target_pairs={{0,8},{8,16},{16,24},{24,32},{32,40},{40,48},{48,56},{56,0},{1,9},... | collective-permute-start | bytes 2359304 | tf_op jit(solution)/shard_map/ppermute | solution.py:18
  123.8 24.5 %collective-permute-start.8 = (bf16[6,4,128,128]{3,2,1,0:T(8,128)(2,1)}, bf16[6,4,128,128]{3,2,1,0:T(8,128)(2,1)}, u32[]{:S(2)}, u32[]{:S(2)}) collective-permute-start(bf16[6,4,128,128]{3,2,1,0:T(8,128)(2,1)} %collective-permute-done.6.refs_5_), channel_id=1, source_target_pairs={{0,56},{8,0},{16,8},{24,16},{32,24},{40,32},{48,40},{56,48},{1,57}... | collective-permute-start | bytes 2359304 | tf_op jit(solution)/shard_map/ppermute | solution.py:18
  142.9 30.2 %all-to-all-start.1 = ((bf16[4,8,3,2,32,128]{5,4,3,2,1,0:T(8,128)(2,1)}), bf16[4,8,3,2,32,128]{5,4,3,2,1,0:T(8,128)(2,1)}, u32[]{:S(2)}, u32[]{:S(2)}) async-start(bf16[4,8,3,2,32,128]{5,4,3,2,1,0:T(8,128)(2,1)} %shard_map.82), calls=%async_computation.1 | async-start | bytes 3145728 | tf_op jit(solution)/shard_map/all_to_all | solution.py:150
  148.3 8.3 %collective-permute-start.10 = (bf16[3,4,128,128]{3,2,1,0:T(8,128)(2,1)S(1)}, bf16[3,4,128,128]{3,2,1,0:T(8,128)(2,1)S(1)}, u32[]{:S(2)}, u32[]{:S(2)}) collective-permute-start(bf16[3,4,128,128]{3,2,1,0:T(8,128)(2,1)S(1)} %slice.33), channel_id=1, source_target_pairs={{0,8},{8,16},{16,24},{24,32},{32,40},{40,48},{48,56},{56,0},{1,9},... | collective-permute-start | bytes 1179656 | tf_op jit(solution)/shard_map/ppermute | solution.py:18
  149.4 7.5 %collective-permute-start.11 = (bf16[3,4,128,128]{3,2,1,0:T(8,128)(2,1)S(1)}, bf16[3,4,128,128]{3,2,1,0:T(8,128)(2,1)S(1)}, u32[]{:S(2)}, u32[]{:S(2)}) collective-permute-start(bf16[3,4,128,128]{3,2,1,0:T(8,128)(2,1)S(1)} %slice.34), channel_id=1, source_target_pairs={{0,56},{8,0},{16,8},{24,16},{32,24},{40,32},{48,40},{56,48},{1,57}... | collective-permute-start | bytes 1179656 | tf_op jit(solution)/shard_map/ppermute | solution.py:18
  173.0 19.2 %all-to-all-start.3 = ((bf16[4,8,3,2,32,128]{5,4,3,2,1,0:T(8,128)(2,1)}), bf16[4,8,3,2,32,128]{5,4,3,2,1,0:T(8,128)(2,1)}, u32[]{:S(2)}, u32[]{:S(2)}) async-start(bf16[4,8,3,2,32,128]{5,4,3,2,1,0:T(8,128)(2,1)} %shard_map.84), calls=%async_computation.3 | async-start | bytes 3145728 | tf_op jit(solution)/shard_map/all_to_all | solution.py:150
  196.9 26.2 %all-to-all-start.4 = ((bf16[8,8,2,32,128]{4,3,2,1,0:T(8,128)(2,1)}), bf16[8,8,2,32,128]{4,3,2,1,0:T(8,128)(2,1)}, u32[]{:S(2)}, u32[]{:S(2)}) async-start(bf16[8,8,2,32,128]{4,3,2,1,0:T(8,128)(2,1)} %pad_maximum_fusion), calls=%async_computation.4 | async-start | bytes 2097152 | tf_op jit(solution)/shard_map/all_to_all | solution.py:153
Sparse Core Ops, SparseCore 0:
  9.2 57.7 all-gather.2

commit v2 on v1

v2 whole, which is shorter than its diff:
```python
import functools

import jax
import jax.numpy as jnp
from jax import lax
from jax.experimental import pallas as pl
from jax.experimental.pallas import tpu as pltpu
from jax.sharding import Mesh
from jax.sharding import PartitionSpec as P

STEPS = (0, 1, -1, 2, -2, 3, -3, 4)
EARLY = 3
CAP = 2
MIB = 1024 * 1024
SMEM = pl.BlockSpec(memory_space=pltpu.SMEM)
VMEM = pl.BlockSpec(memory_space=pltpu.VMEM)
ANY = pl.BlockSpec(memory_space=pl.ANY)
CLOCK = 5 * 10**9


def shift(array, axis, by):
    count = lax.axis_size(axis)
    return lax.ppermute(array, axis, [(i, (i + by) % count) for i in range(count)])


def hold(*refs):
    pass


def after_these(arrays, others, flops=0):
    return pl.pallas_call(
        hold,
        out_shape=[jax.ShapeDtypeStruct(a.shape, a.dtype) for a in arrays],
        in_specs=[ANY] * (len(arrays) + len(others)),
        out_specs=[ANY] * len(arrays),
        input_output_aliases={i: i for i in range(len(arrays))},
        cost_estimate=pl.CostEstimate(flops=flops, bytes_accessed=0, transcendentals=0),
    )(*arrays, *others)


def first_and_last(hit, keys, top):
    return jnp.stack(
        [jnp.min(jnp.where(hit, keys, top), -1), jnp.max(jnp.where(hit, keys, 0), -1)], -1
    )


def slot_of(tile, partner, place, seen, z):
    owner = lax.div(partner[tile], 6)
    lane = (owner >> 4) * 2 + (owner & 1)
    step = place[((owner >> 1) - z) & 7]
    rank = seen[owner]
    seen[owner] = rank + 1
    return lane, step, rank


def clear(seen):
    def one(i, _):
        seen[i] = 0
        return 0

    lax.fori_loop(0, seen.shape[0], one, 0)


def send_kernel(spot, place, partner, left_dims, right_dims, psi, early, late, seen):
    z, y = spot[0], spot[1]
    tiles, size, _ = psi.shape
    rows = early.shape[-2]
    pairs = tiles // left_dims.shape[0]
    row = lax.broadcasted_iota(jnp.int32, (size, size), 0)
    column = lax.broadcasted_iota(jnp.int32, (size, size), 1)
    start = pl.multiple_of(y * rows, rows)
    clear(seen)

    def one_tile(tile, _):
        lane, step, rank = slot_of(tile, partner, place, seen, z)
        height, width = left_dims[lax.div(tile, pairs)], right_dims[partner[tile]]

        @pl.when(step < EARLY)
        def _():
            keep = (row[:rows] < height - start) & (column[:rows] < width)
            values = psi[tile, pl.ds(start, rows)].astype(jnp.float32)
            early[lane, step, rank] = jnp.where(keep, values, 0.0).astype(psi.dtype)

        @pl.when(step >= EARLY)
        def _():
            keep = (row < height) & (column < width)
            values = psi[tile].astype(jnp.float32)
            late[lane, step - EARLY, rank] = jnp.where(keep, values, 0.0).astype(psi.dtype)

        return 0

    lax.fori_loop(0, tiles, one_tile, 0)


def chunk_kernel(first, count, begin, quarters, halves, relative, spot, left_at, right_at, *refs):
    refs = list(refs)
    lefts = [refs.pop(0) for _ in range(8)]
    sent = [refs.pop(0) for _ in range(quarters)]
    rights = [[refs.pop(0) for _ in range(parts)] for parts in halves]
    out, left, right, psi, total, flags = refs[-6:]
    x, y, k = spot[3], spot[1], spot[2]
    terms, size = left.shape[1], left.shape[-1]
    rows = size // 4
    copies = []

    def copy(source, there):
        copies.append(pltpu.make_async_copy(source, there, flags.at[len(copies)]))
        copies[-1].start()

    for step, parts in enumerate(rights):
        start = 0
        for part in parts:
            copy(part, right.at[step, pl.ds(start, part.shape[0])])
            start += part.shape[0]
    for away, part in enumerate(sent):
        if quarters == 4:
            row = pl.multiple_of(lax.rem(y + away, 4) * rows, rows)
            copy(part, psi.at[:, :, :, pl.ds(row, rows)])
        else:
            copy(part.at[:, pl.ds(begin, count)], psi)
    groups = ((0, 2), (2, 8))
    for low, high in groups:
        for away in range(low, high):
            copy(lefts[away], left.at[away])
    for ready in copies[:-8]:
        ready.wait()
    for low, high in groups:
        for away in range(low, high):
            copies[-8:][away].wait()
        for away in range(low, high):
            lane = lax.rem(x + away // 2, 4) * 2 + (k if away % 2 == 0 else 1 - k)
            for step in range(count):
                for rank in range(CAP):
                    slot = (lane * len(STEPS) + first + step) * CAP + rank
                    i, j = left_at[slot], right_at[slot]
                    stack = jnp.concatenate([left[away, term, i] for term in range(terms)], 0)
                    product = jnp.dot(
                        stack, psi[lane, step, rank], preferred_element_type=jnp.float32
                    ).astype(jnp.bfloat16)
                    side = [product[term * size : (term + 1) * size] for term in range(terms)]
                    other = jnp.concatenate([right[step, term, j] for term in range(terms)], 1)
                    total[lane, step, rank] = lax.dot_general(
                        jnp.concatenate(side, 1),
                        other,
                        (((1,), (1,)), ((), ())),
                        preferred_element_type=jnp.float32,
                    ).astype(jnp.bfloat16)
    copies.clear()
    for far in range(4):
        quarter = lax.rem(y + far, 4) if relative else far
        row = pl.multiple_of(quarter * rows, rows)
        copy(total.at[:, :, :, pl.ds(row, rows)], out.at[far])
    for ready in copies:
        ready.wait()


def compute_chunk(first, count, begin, spot, left_at, right_at, lefts, sent, rights, after, relative):
    sources = len(lefts)
    terms, sectors, size, _ = lefts[0].shape
    rows, slots = size // 4, sources * count * CAP
    quarters, halves = len(sent), [len(parts) for parts in rights]
    flat = [part for parts in rights for part in parts]
    return pl.pallas_call(
        functools.partial(chunk_kernel, first, count, begin, quarters, halves, relative),
        out_shape=jax.ShapeDtypeStruct((4, sources, count, CAP, rows, size), jnp.bfloat16),
        in_specs=[SMEM] * 3 + [ANY] * (8 + quarters + len(flat) + len(after)),
        out_specs=ANY,
        scratch_shapes=[
            pltpu.VMEM((sources, terms, sectors, size, size), jnp.bfloat16),
            pltpu.VMEM((count, terms, sectors, size, size), jnp.bfloat16),
            pltpu.VMEM((sources, count, CAP, size, size), jnp.bfloat16),
            pltpu.VMEM((sources, count, CAP, size, size), jnp.bfloat16),
            pltpu.SemaphoreType.DMA((8 + quarters + len(flat),)),
        ],
        compiler_params=pltpu.CompilerParams(vmem_limit_bytes=56 * MIB),
        cost_estimate=pl.CostEstimate(
            flops=slots * terms * 4 * size**3 * 6,
            bytes_accessed=slots * size * size * 4,
            transcendentals=0,
        ),
    )(spot, left_at, right_at, *lefts, *sent, *flat, *after)


def finish_kernel(spot, place, partner, left_dims, right_dims, *refs):
    parts, (out, seen) = refs[:2], refs[2:]
    z, y = spot[0], spot[1]
    tiles, rows, size = out.shape
    pairs = tiles // left_dims.shape[0]
    row = lax.broadcasted_iota(jnp.int32, (rows, size), 0) + y * rows
    column = lax.broadcasted_iota(jnp.int32, (rows, size), 1)
    clear(seen)

    def one_tile(tile, _):
        lane, step, rank = slot_of(tile, partner, place, seen, z)
        keep = (row < left_dims[lax.div(tile, pairs)]) & (column < right_dims[partner[tile]])
        start = 0
        for part in parts:
            planes, count = part.shape[0] // 8, part.shape[1]

            @pl.when((step >= start) & (step < start + count))
            def _(part=part, planes=planes, start=start):
                whole = part[lane, step - start, rank].astype(jnp.float32)
                for plane in range(1, planes):
                    whole += part[plane * 8 + lane, step - start, rank].astype(jnp.float32)
                out[tile] = jnp.where(keep, whole, 0.0).astype(out.dtype)

            start += count
        return 0

    lax.fori_loop(0, tiles, one_tile, 0)


def on_device(wavefunction, left_env, right_env, left_dims, right_dims, partner):
    sectors, pairs, size, _ = wavefunction.shape
    tiles = sectors * pairs
    x, z, k, y = (lax.axis_index(name) for name in ("x", "z", "k", "y"))
    nx, nz, nk, ny = (lax.axis_size(name) for name in ("x", "z", "k", "y"))
    rows, lanes, many = size // ny, nx * nk, len(STEPS)
    steps = jnp.array(STEPS, jnp.int32)
    place = jnp.array([STEPS.index(d if d <= 4 else d - nz) for d in range(nz)], jnp.int32)
    spot = jnp.stack([z, y, k, x]).astype(jnp.int32)

    def both_ways(arrays):
        return shift(arrays[0], "z", 1), shift(arrays[1], "z", -1)

    one = both_ways((right_env, right_env))
    block = (x * nz + z) * nk + k
    own_partner = lax.dynamic_slice_in_dim(partner, block * sectors, sectors, 0).reshape(tiles)
    own_dims = lax.dynamic_slice_in_dim(left_dims, block * sectors, sectors, 0)
    own = (spot, place, own_partner, own_dims, right_dims)
    counters = [pltpu.SMEM((nx * nz * nk,), jnp.int32)]
    early, late = pl.pallas_call(
        send_kernel,
        out_shape=[
            jax.ShapeDtypeStruct((lanes, EARLY, CAP, rows, size), jnp.bfloat16),
            jax.ShapeDtypeStruct((lanes, many - EARLY, CAP, size, size), jnp.bfloat16),
        ],
        in_specs=[SMEM] * 5 + [VMEM],
        out_specs=[VMEM, VMEM],
        scratch_shapes=counters,
        compiler_params=pltpu.CompilerParams(vmem_limit_bytes=20 * MIB),
    )(*own, wavefunction.reshape(tiles, size, size))
    one = after_these(one, (early, late), CLOCK)
    two = both_ways(one)
    after, before = shift(left_env, "x", -1), shift(left_env, "x", 1)
    lefts = [left_env, after, shift(before, "x", 1), before]
    lefts = [both for own in lefts for both in (own, shift(own, "k", 1))]
    early = lax.all_to_all(early, ("x", "k"), 0, 0, tiled=True)
    late = [lax.all_to_all(late, ("x", "k"), 0, 0, tiled=True)]
    (early,) = after_these((early,), (*one, lefts[3], lefts[7]))
    after, before = shift(early, "y", -1), shift(early, "y", 1)
    two = after_these(two, (after, before, lefts[1]), CLOCK)
    three = both_ways(two)
    early = [early, after, shift(before, "y", 1), before]

    group = lax.dynamic_index_in_dim(partner.reshape(nx, nz, nk, tiles), z, 1, keepdims=False)
    group = group.reshape(lanes, 1, tiles)
    order = jnp.arange(tiles, dtype=jnp.int32)
    wanted = ((x * nz + (z + steps) % nz) * nk + k)[None, :, None]
    keys = first_and_last(
        group // sectors == wanted, order * 8 + group % sectors, (tiles - 1) * 8 + sectors - 1
    ).reshape(-1)
    left_at, right_at = keys // (8 * pairs), jnp.minimum(keys % 8, sectors - 1)

    def chunk(first, stop, sent, after, relative=False):
        begin = 0 if first < EARLY else first - EARLY
        return compute_chunk(
            first, stop - first, begin, spot, left_at, right_at, lefts, sent, rights[first:stop], after, relative
        )

    def straight_back(partial):
        partial = partial.reshape(ny * lanes, *partial.shape[2:])
        return lax.all_to_all(partial, ("y", "x", "k"), 0, 0, tiled=True)

    rights = [[right_env], *[[two_way] for two_way in (one[1], one[0])]]
    first = chunk(0, EARLY, early, [*two])
    three = after_these(three, (first,), CLOCK)
    half = right_env.shape[0] // 2
    four = both_ways((three[0][:half], three[1][half:]))
    (held,) = after_these((first,), late)
    first_back = straight_back(held)
    rights += [[two[1]], [two[0]], [three[1]], [three[0]], [*four]]
    second = chunk(EARLY, many, late, [first])
    second_back = straight_back(second)
    out = pl.pallas_call(
        finish_kernel,
        out_shape=jax.ShapeDtypeStruct((tiles, rows, size), jnp.bfloat16),
        in_specs=[SMEM] * 5 + [VMEM] * 2,
        out_specs=VMEM,
        scratch_shapes=counters,
        compiler_params=pltpu.CompilerParams(vmem_limit_bytes=20 * MIB),
    )(*own, first_back, second_back)
    return out.reshape(sectors, pairs, rows, size)


def solution(mesh):
    fine = Mesh(mesh.devices.reshape(4, 8, 2, 4), ("x", "z", "k", "y"))
    blk = ("x", "z", "k")
    placed = (P(blk), P("y", blk), P("y", blk), P(), P(), P())
    return jax.shard_map(
        on_device, mesh=fine, in_specs=placed, out_specs=P(blk, None, "y", None), check_vma=False
    )
```

time: 236 us -> 157 us (0.67)
  waiting for transfers between devices: 55.1 us -> 28.8 us
  local copies, waits for them, and re-layouts: 31 us -> 13.7 us
  other arithmetic: 15.2 us -> 1.16 us
  between operations: 13.7 us -> 0.21 us
  Pallas kernels: 44.5 us -> 31.6 us
  blocking collectives: 32.3 us -> 40.1 us
    all_to_all x4 -> x3, waiting for transfers between devices: 25.2 us -> 11.9 us  [the longest x1 10.4 us: straight_back(): return lax.all_to_all(partial, ('y', 'x', 'k'), 0, 0, tiled=True)]
    pallas_call x3 -> x9, Pallas kernels: 44.5 us -> 31.6 us  [the longest x2 20.2 us: compute_chunk(): pl.pallas_call(functools.partial(chunk_kernel, first, count, begin, quart...]
    ppermute x12 -> x18, waiting for transfers between devices: 29.2 us -> 16.9 us  [shift(): lax.ppermute(array, axis, [(i, (i + by) % count) for i in range(count)])]
    all_to_all x4 -> x3, starting transfers between devices: 23.9 us -> 14.3 us  [the longest x1 6.03 us: straight_back(): return lax.all_to_all(partial, ('y', 'x', 'k'), 0, 0, tiled=True)]
    all_gather x1 -> x0, local copies, waits for them, and re-layouts: 8 us -> none  [on_device(): left_all = lax.all_gather(jnp.swapaxes(left_env, 0, 1), ('x', 'k'))]
    all_to_all x1, blocking collectives: 32.3 us -> 40.1 us  [straight_back(): return lax.all_to_all(partial, ('y', 'x', 'k'), 0, 0, tiled=True)]
    gather x4 -> x0, local copies, waits for them, and re-layouts: 7.3 us -> none  [the longest x1 2.79 us: on_device(): own = jnp.take(returned, spot, axis=0, mode='clip') * mask]
    ppermute x12 -> x18, starting transfers between devices: 19.5 us -> 26.8 us  [shift(): lax.ppermute(array, axis, [(i, (i + by) % count) for i in range(count)])]
  transfers between devices with their start and end apart: 17 -> 21, of which waited for: 6 -> 5; matrix products, arithmetic and copies ran while one was open for 15% -> 4% of each run, Pallas kernels for 14% -> 17%
where the time goes in v2:
time: 157 us
  starting transfers between devices  41.1 us (26%)
  blocking collectives  40.1 us (26%)
  Pallas kernels  31.6 us (20%)
  waiting for transfers between devices  28.8 us (18%)
  local copies, waits for them, and re-layouts  13.7 us (9%)
    all_to_all x1, blocking collectives, straight_back(): return lax.all_to_all(partial, ('y', 'x', 'k'), 0, 0, tiled=True)  40.1 us
    ppermute x18, starting transfers between devices, shift(): lax.ppermute(array, axis, [(i, (i + by) % count) for i in range(count)])  26.8 us
    pallas_call x2, Pallas kernels, compute_chunk(): pl.pallas_call(functools.partial(chunk_kernel, first, count, begin, quart...  20.2 us
    ppermute x18, waiting for transfers between devices, shift(): lax.ppermute(array, axis, [(i, (i + by) % count) for i in range(count)])  16.9 us
    all_to_all x1, waiting for transfers between devices, straight_back(): return lax.all_to_all(partial, ('y', 'x', 'k'), 0, 0, tiled=True)  10.4 us
    unnamed x36, local copies, waits for them, and re-layouts  9.43 us
    all_to_all x1, starting transfers between devices, straight_back(): return lax.all_to_all(partial, ('y', 'x', 'k'), 0, 0, tiled=True)  6.03 us
    pallas_call x1, Pallas kernels, on_device(): pl.pallas_call(send_kernel, out_shape=[jax.ShapeDtypeStruct((lanes, EARLY...  5.89 us
  transfers between devices with their start and end apart: 21, of which 5 were waited for; matrix products, arithmetic and copies ran while one was open for 4% of the time, Pallas kernels for 17%

profile of v2, /device:TPU:1, one launch (start us, length us, event | category | flops | bytes accessed | tf_op | source)
XLA Modules:
  0.0 156.7 jit_solution(18411478897076735111)
XLA Ops:
  0.0 2.0 %collective-permute-start.3 = (bf16[4,6,128,128]{3,2,1,0:T(8,128)(2,1)}, bf16[4,6,128,128]{3,2,1,0:T(8,128)(2,1)}, u32[]{:S(2)}, u32[]{:S(2)}) collective-permute-start(bf16[4,6,128,128]{3,2,1,0:T(8,128)(2,1)} %refs_0_.3), channel_id=1, source_target_pairs={{0,64},{64,128},{128,192},{192,0},{1,65},{65,129},{129,193},{193,1... | collective-permute-start | bytes 2359304 | tf_op jit(solution)/shard_map/ppermute | solution.py:23
  2.0 1.6 %collective-permute-start.7 = (bf16[4,6,128,128]{3,2,1,0:T(8,128)(2,1)}, bf16[4,6,128,128]{3,2,1,0:T(8,128)(2,1)S(1)}, u32[]{:S(2)}, u32[]{:S(2)}) collective-permute-start(bf16[4,6,128,128]{3,2,1,0:T(8,128)(2,1)} %refs_12_.1), channel_id=1, source_target_pairs={{0,8},{8,16},{16,24},{24,32},{32,40},{40,48},{48,56},{56,0},{1,9},... | collective-permute-start | bytes 2359304 | tf_op jit(solution)/shard_map/ppermute | solution.py:23
  3.7 1.5 collective-permute-start.1
  5.1 3.9 %collective-permute-start.8 = (bf16[4,6,128,128]{3,2,1,0:T(8,128)(2,1)}, bf16[4,6,128,128]{3,2,1,0:T(8,128)(2,1)S(1)}, u32[]{:S(2)}, u32[]{:S(2)}) collective-permute-start(bf16[4,6,128,128]{3,2,1,0:T(8,128)(2,1)} %refs_12_.1), channel_id=1, source_target_pairs={{0,56},{8,0},{16,8},{24,16},{32,24},{40,32},{48,40},{56,48},{1,57}... | collective-permute-start | bytes 2359304 | tf_op jit(solution)/shard_map/ppermute | solution.py:23
  9.1 1.5 collective-permute-start
  10.6 0.8 dynamic_slice.11.left_dims
  11.4 0.8 constant_dynamic-slice_fusion
  12.2 0.1 copy.22
  12.2 0.1 reshape.96.partner
  12.3 0.1 pad_add_fusion.1.spot
  12.4 1.9 %copy-done = bf16[6,16,128,128]{3,2,1,0:T(8,128)(2,1)S(1)} copy-done((bf16[6,16,128,128]{3,2,1,0:T(8,128)(2,1)S(1)}, bf16[6,16,128,128]{3,2,1,0:T(8,128)(2,1)}, u32[]{:S(2)}) %copy-start) | copy-done | bytes 3145752
  14.3 0.7 copy-done.1
  15.0 0.7 copy-done.5
  15.6 5.9 %shard_map.82 = (bf16[8,3,2,32,128]{4,3,2,1,0:T(8,128)(2,1)}, bf16[8,5,2,128,128]{4,3,2,1,0:T(8,128)(2,1)}) custom-call(s32[4]{0:T(128)S(1)} %pad_add_fusion.1.spot, s32[8]{0:T(128)S(1)} %copy-done.5, s32[96]{0:T(128)S(1)} %reshape.96.partner, s32[6]{0:T(128)S(1)} %dynamic_slice.11.left_dims, s32[384]{0:T(512)S(1)} %copy-done.1, ...), custom_call_target="tpu_custom_call" | custom-call | tf_op jit(solution)/shard_map/pallas_call | solution.py:232
  21.5 3.4 %all-to-all-start = ((bf16[8,3,2,32,128]{4,3,2,1,0:T(8,128)(2,1)}), bf16[8,3,2,32,128]{4,3,2,1,0:T(8,128)(2,1)S(1)}, u32[]{:S(2)}, u32[]{:S(2)}) async-start(bf16[8,3,2,32,128]{4,3,2,1,0:T(8,128)(2,1)} %get-tuple-element.13.refs_2_), calls=%async_computation | async-start | bytes 786432 | tf_op jit(solution)/shard_map/all_to_all | solution.py:248
  24.9 0.1 copy.23
  25.1 0.1 reshape.97
  25.2 0.0 collective-permute-done.3.refs_6_
  25.3 0.1 collective-permute-start.6
  25.4 0.0 collective-permute-done.7.refs_0_
  25.4 1.7 %collective-permute-start.4 = (bf16[4,6,128,128]{3,2,1,0:T(8,128)(2,1)}, bf16[4,6,128,128]{3,2,1,0:T(8,128)(2,1)}, u32[]{:S(2)}, u32[]{:S(2)}) collective-permute-start(bf16[4,6,128,128]{3,2,1,0:T(8,128)(2,1)} %collective-permute-done.3.refs_6_), channel_id=1, source_target_pairs={{0,64},{64,128},{128,192},{192,0},{1,65},{65,129},{129,193},{193,1... | collective-permute-start | bytes 2359304 | tf_op jit(solution)/shard_map/ppermute | solution.py:23
  27.1 0.0 collective-permute-done.1.refs_2_
  27.1 0.7 collective-permute-start.2
  27.8 0.0 collective-permute-done.8.refs_1_
  27.8 0.9 copy-done.12
  28.8 0.0 collective-permute-start.12
  28.8 0.0 collective-permute-done.6.refs_4_.refs_7_
  28.8 0.0 copy-start.10
  28.8 2.7 %collective-permute-start.13 = (bf16[4,6,128,128]{3,2,1,0:T(8,128)(2,1)}, bf16[4,6,128,128]{3,2,1,0:T(8,128)(2,1)}, u32[]{:S(2)}, u32[]{:S(2)}) collective-permute-start(bf16[4,6,128,128]{3,2,1,0:T(8,128)(2,1)} %get-tuple-element.16.refs_2_.refs_13_), channel_id=1, source_target_pairs={{0,56},{8,0},{16,8},{24,16},{32,24},{40,32},{48,40},{56,48},{1,57}... | collective-permute-start | bytes 2359304 | tf_op jit(solution)/shard_map/ppermute | solution.py:23
  31.5 1.5 all-to-all-done.refs_0_
  33.0 0.8 copy-done.9
  33.7 4.9 %all-to-all-start.1 = ((bf16[8,5,2,128,128]{4,3,2,1,0:T(8,128)(2,1)}), bf16[8,5,2,128,128]{4,3,2,1,0:T(8,128)(2,1)S(1)}, u32[]{:S(2)}, u32[]{:S(2)}) async-start(bf16[8,5,2,128,128]{4,3,2,1,0:T(8,128)(2,1)} %get-tuple-element.14.refs_3_), calls=%async_computation.1 | async-start | bytes 5242880 | tf_op jit(solution)/shard_map/all_to_all | solution.py:249
  38.6 0.0 collective-permute-done.2.refs_3_
  38.6 1.3 collective-permute-start.10
  39.9 0.0 collective-permute-done.refs_4_.refs_1_
  39.9 1.5 collective-permute-start.9
  41.4 0.4 fusion
  41.9 7.9 %collective-permute-done.4.refs_4_ = bf16[4,6,128,128]{3,2,1,0:T(8,128)(2,1)} collective-permute-done((bf16[4,6,128,128]{3,2,1,0:T(8,128)(2,1)}, bf16[4,6,128,128]{3,2,1,0:T(8,128)(2,1)}, u32[]{:S(2)}, u32[]{:S(2)}) %collective-permute-start.4) | collective-permute-done | bytes 786464 | tf_op jit(solution)/shard_map/ppermute | solution.py:23
  49.8 1.5 collective-permute-start.5
  51.3 0.1 copy.24
  51.4 0.1 reshape.98
  51.5 0.6 fusion.7
  52.1 0.0 collective-permute-done.10.refs_3_.refs_11_
  52.1 1.3 collective-permute-start.11
  53.4 0.0 collective-permute-done.12.refs_0_
  53.4 0.0 collective-permute-done.13.refs_1_
  53.5 0.7 copy-done.16
  54.2 2.7 %collective-permute-start.15 = (bf16[4,6,128,128]{3,2,1,0:T(8,128)(2,1)}, bf16[4,6,128,128]{3,2,1,0:T(8,128)(2,1)}, u32[]{:S(2)}, u32[]{:S(2)}) collective-permute-start(bf16[4,6,128,128]{3,2,1,0:T(8,128)(2,1)} %get-tuple-element.18.refs_16_.refs_9_), channel_id=1, source_target_pairs={{0,56},{8,0},{16,8},{24,16},{32,24},{40,32},{48,40},{56,48},{1,57}... | collective-permute-start | bytes 2359304 | tf_op jit(solution)/shard_map/ppermute | solution.py:23
  56.9 7.7 %collective-permute-done.11.refs_10_ = bf16[8,3,2,32,128]{4,3,2,1,0:T(8,128)(2,1)} collective-permute-done((bf16[8,3,2,32,128]{4,3,2,1,0:T(8,128)(2,1)}, bf16[8,3,2,32,128]{4,3,2,1,0:T(8,128)(2,1)}, u32[]{:S(2)}, u32[]{:S(2)}) %collective-permute-start.11) | collective-permute-done | bytes 393248 | tf_op jit(solution)/shard_map/ppermute | solution.py:23
  64.5 8.6 %shard_map.86.refs_2_.refs_15_ = bf16[4,8,3,2,32,128]{5,4,3,2,1,0:T(8,128)(2,1)} custom-call(s32[4]{0:T(128)} %copy-done.3, s32[128]{0:T(128)} %get-tuple-element.28.left_at, s32[128]{0:T(128)} %get-tuple-element.27.right_at, bf16[4,6,128,128]{3,2,1,0:T(8,128)(2,1)} %refs_0_.3, bf16[4,6,128,128]{3,2,1,0:T(8,128)(2,1)} %collective-permute-done.refs_4_.refs_1_, ...), custom_call_target="tpu_custom_call" | custom-call | flops 9663676416 | bytes 3145728 | tf_op jit(solution)/shard_map/pallas_call | solution.py:163
  73.2 1.3 collective-permute-done.14.refs_0_
  74.5 0.9 copy-done.13
  75.4 1.1 slice.7
  76.5 1.0 slice.6
  77.5 0.1 collective-permute-start.16
  77.6 2.7 %collective-permute-start.17 = (bf16[2,6,128,128]{3,2,1,0:T(8,128)(2,1)S(1)}, bf16[2,6,128,128]{3,2,1,0:T(8,128)(2,1)}, u32[]{:S(2)}, u32[]{:S(2)}) collective-permute-start(bf16[2,6,128,128]{3,2,1,0:T(8,128)(2,1)S(1)} %slice.7), channel_id=1, source_target_pairs={{0,56},{8,0},{16,8},{24,16},{32,24},{40,32},{48,40},{56,48},{1,57}... | collective-permute-start | bytes 1179656 | tf_op jit(solution)/shard_map/ppermute | solution.py:23
  80.3 1.2 copy.30.refs_0_
  81.5 1.5 copy-done.7
  83.0 6.0 %all-to-all-start.2 = ((bf16[32,3,2,32,128]{4,3,2,1,0:T(8,128)(2,1)}), bf16[32,3,2,32,128]{4,3,2,1,0:T(8,128)(2,1)S(1)}, u32[]{:S(2)}, u32[]{:S(2)}) async-start(bf16[32,3,2,32,128]{4,3,2,1,0:T(8,128)(2,1)} %bitcast.13), calls=%async_computation.2 | async-start | bytes 3145728 | tf_op jit(solution)/shard_map/all_to_all | solution.py:273
  89.1 0.0 collective-permute-done.17.refs_14_
  89.1 11.6 %shard_map.89 = bf16[4,8,5,2,32,128]{5,4,3,2,1,0:T(8,128)(2,1)} custom-call(s32[4]{0:T(128)} %copy-done.3, s32[128]{0:T(128)} %get-tuple-element.28.left_at, s32[128]{0:T(128)} %get-tuple-element.27.right_at, bf16[4,6,128,128]{3,2,1,0:T(8,128)(2,1)} %refs_0_.3, bf16[4,6,128,128]{3,2,1,0:T(8,128)(2,1)} %collective-permute-done.refs_4_.refs_1_, ...), custom_call_target="tpu_custom_call" | custom-call | flops 16106127360 | bytes 5242880 | tf_op jit(solution)/shard_map/pallas_call | solution.py:163
  100.7 10.4 %all-to-all-done.2.refs_0_ = bf16[32,3,2,32,128]{4,3,2,1,0:T(8,128)(2,1)S(1)} async-done(((bf16[32,3,2,32,128]{4,3,2,1,0:T(8,128)(2,1)}), bf16[32,3,2,32,128]{4,3,2,1,0:T(8,128)(2,1)S(1)}, u32[]{:S(2)}, u32[]{:S(2)}) %all-to-all-start.2) | async-done | bytes 1572896 | tf_op jit(solution)/shard_map/all_to_all | solution.py:273
  111.1 40.1 %all_to_all.20.refs_1_ = bf16[32,5,2,32,128]{4,3,2,1,0:T(8,128)(2,1)S(1)} all-to-all(bf16[32,5,2,32,128]{4,3,2,1,0:T(8,128)(2,1)} %bitcast.14), channel_id=1, replica_groups=mesh['x'=4,'z'=8,'k'=2,'y'=4] {'y','x','k'}, dimensions={0} | all-to-all | bytes 5242880 | tf_op jit(solution)/shard_map/all_to_all | solution.py:273
  151.2 5.5 %shard_map.90 = bf16[96,32,128]{2,1,0:T(8,128)(2,1)} custom-call(s32[4]{0:T(128)S(1)} %copy-done.4, s32[8]{0:T(128)S(1)} %copy-done.6, s32[96]{0:T(128)S(1)} %reshape.96.partner, s32[6]{0:T(128)S(1)} %dynamic_slice.11.left_dims, s32[384]{0:T(512)S(1)} %copy-done.2, bf16[32,3,2,32,128]{4,3,2,1,0:T(8,128)(2,1)S(1)} %all-to-all-done.2.refs_0_, ...), custom_call_target="tpu_custom_call" | custom-call | tf_op jit(solution)/shard_map/pallas_call | solution.py:285
  (43 shorter events, 0.1 us)
Async XLA Ops:
  0.0 25.4 %copy-start.15 = (s32[8]{0:T(128)S(1)}, s32[8]{0:T(128)}, u32[]{:S(2)}) copy-start(s32[8]{0:T(128)} %constant.94.clone) | copy-start | bytes 100
  0.0 24.9 %copy-start.14 = (s32[384,16]{0,1:T(8,128)S(1)}, s32[384,16]{0,1:T(8,128)}, u32[]{:S(2)}) copy-start(s32[384,16]{0,1:T(8,128)} %param.13) | copy-start | bytes 73732
  0.0 25.2 %collective-permute-start.3 = (bf16[4,6,128,128]{3,2,1,0:T(8,128)(2,1)}, bf16[4,6,128,128]{3,2,1,0:T(8,128)(2,1)}, u32[]{:S(2)}, u32[]{:S(2)}) collective-permute-start(bf16[4,6,128,128]{3,2,1,0:T(8,128)(2,1)} %refs_0_.3), channel_id=1, source_target_pairs={{0,64},{64,128},{128,192},{192,0},{1,65},{65,129},{129,193},{193,1... | collective-permute-start | bytes 2359304 | tf_op jit(solution)/shard_map/ppermute | solution.py:23
  2.0 23.4 %collective-permute-start.7 = (bf16[4,6,128,128]{3,2,1,0:T(8,128)(2,1)}, bf16[4,6,128,128]{3,2,1,0:T(8,128)(2,1)S(1)}, u32[]{:S(2)}, u32[]{:S(2)}) collective-permute-start(bf16[4,6,128,128]{3,2,1,0:T(8,128)(2,1)} %refs_12_.1), channel_id=1, source_target_pairs={{0,8},{8,16},{16,24},{24,32},{32,40},{40,48},{48,56},{56,0},{1,9},... | collective-permute-start | bytes 2359304 | tf_op jit(solution)/shard_map/ppermute | solution.py:23
  3.7 23.5 %collective-permute-start.1 = (bf16[4,6,128,128]{3,2,1,0:T(8,128)(2,1)}, bf16[4,6,128,128]{3,2,1,0:T(8,128)(2,1)}, u32[]{:S(2)}, u32[]{:S(2)}) collective-permute-start(bf16[4,6,128,128]{3,2,1,0:T(8,128)(2,1)} %refs_0_.3), channel_id=1, source_target_pairs={{0,192},{64,0},{128,64},{192,128},{1,193},{65,1},{129,65},{193,129... | collective-permute-start | bytes 2359304 | tf_op jit(solution)/shard_map/ppermute | solution.py:23
  5.1 22.7 %collective-permute-start.8 = (bf16[4,6,128,128]{3,2,1,0:T(8,128)(2,1)}, bf16[4,6,128,128]{3,2,1,0:T(8,128)(2,1)S(1)}, u32[]{:S(2)}, u32[]{:S(2)}) collective-permute-start(bf16[4,6,128,128]{3,2,1,0:T(8,128)(2,1)} %refs_12_.1), channel_id=1, source_target_pairs={{0,56},{8,0},{16,8},{24,16},{32,24},{40,32},{48,40},{56,48},{1,57}... | collective-permute-start | bytes 2359304 | tf_op jit(solution)/shard_map/ppermute | solution.py:23
  9.1 30.8 %collective-permute-start = (bf16[4,6,128,128]{3,2,1,0:T(8,128)(2,1)}, bf16[4,6,128,128]{3,2,1,0:T(8,128)(2,1)}, u32[]{:S(2)}, u32[]{:S(2)}) collective-permute-start(bf16[4,6,128,128]{3,2,1,0:T(8,128)(2,1)} %refs_0_.3), channel_id=1, source_target_pairs={{0,4},{4,0},{1,5},{5,1},{2,6},{6,2},{3,7},{7,3},{8,12},{12,8},{9,1... | collective-permute-start | bytes 2359304 | tf_op jit(solution)/shard_map/ppermute | solution.py:23
  12.4 16.4 %copy-start.3 = (s32[4]{0:T(128)}, s32[4]{0:T(128)S(1)}, u32[]{:S(2)}) copy-start(s32[4]{0:T(128)S(1)} %pad_add_fusion.1.spot) | copy-start | bytes 52
  12.4 1.9 %copy-start = (bf16[6,16,128,128]{3,2,1,0:T(8,128)(2,1)S(1)}, bf16[6,16,128,128]{3,2,1,0:T(8,128)(2,1)}, u32[]{:S(2)}) copy-start(bf16[6,16,128,128]{3,2,1,0:T(8,128)(2,1)} %param.8) | copy-start | bytes 9437188
  14.3 0.7 copy-start.1
  15.0 0.7 copy-start.5
  21.5 11.5 %all-to-all-start = ((bf16[8,3,2,32,128]{4,3,2,1,0:T(8,128)(2,1)}), bf16[8,3,2,32,128]{4,3,2,1,0:T(8,128)(2,1)S(1)}, u32[]{:S(2)}, u32[]{:S(2)}) async-start(bf16[8,3,2,32,128]{4,3,2,1,0:T(8,128)(2,1)} %get-tuple-element.13.refs_2_), calls=%async_computation | async-start | bytes 786432 | tf_op jit(solution)/shard_map/all_to_all | solution.py:248
  25.3 3.5 %collective-permute-start.6 = (bf16[4,6,128,128]{3,2,1,0:T(8,128)(2,1)}, bf16[4,6,128,128]{3,2,1,0:T(8,128)(2,1)S(1)}, u32[]{:S(2)}, u32[]{:S(2)}) collective-permute-start(bf16[4,6,128,128]{3,2,1,0:T(8,128)(2,1)} %collective-permute-done.3.refs_6_), channel_id=1, source_target_pairs={{0,4},{4,0},{1,5},{5,1},{2,6},{6,2},{3,7},{7,3},{8,12},{12,8},{9,1... | collective-permute-start | bytes 2359304 | tf_op jit(solution)/shard_map/ppermute | solution.py:23
  25.4 2.4 %copy-start.11 = (bf16[4,6,128,128]{3,2,1,0:T(8,128)(2,1)}, bf16[4,6,128,128]{3,2,1,0:T(8,128)(2,1)S(1)}, u32[]{:S(2)}) copy-start(bf16[4,6,128,128]{3,2,1,0:T(8,128)(2,1)S(1)} %collective-permute-done.7.refs_0_) | copy-start | bytes 2359300
  25.4 24.4 %collective-permute-start.4 = (bf16[4,6,128,128]{3,2,1,0:T(8,128)(2,1)}, bf16[4,6,128,128]{3,2,1,0:T(8,128)(2,1)}, u32[]{:S(2)}, u32[]{:S(2)}) collective-permute-start(bf16[4,6,128,128]{3,2,1,0:T(8,128)(2,1)} %collective-permute-done.3.refs_6_), channel_id=1, source_target_pairs={{0,64},{64,128},{128,192},{192,0},{1,65},{65,129},{129,193},{193,1... | collective-permute-start | bytes 2359304 | tf_op jit(solution)/shard_map/ppermute | solution.py:23
  27.1 11.5 %collective-permute-start.2 = (bf16[4,6,128,128]{3,2,1,0:T(8,128)(2,1)}, bf16[4,6,128,128]{3,2,1,0:T(8,128)(2,1)}, u32[]{:S(2)}, u32[]{:S(2)}) collective-permute-start(bf16[4,6,128,128]{3,2,1,0:T(8,128)(2,1)} %collective-permute-done.1.refs_2_), channel_id=1, source_target_pairs={{0,4},{4,0},{1,5},{5,1},{2,6},{6,2},{3,7},{7,3},{8,12},{12,8},{9,1... | collective-permute-start | bytes 2359304 | tf_op jit(solution)/shard_map/ppermute | solution.py:23
  27.8 0.9 copy-start.12
  28.8 24.7 %collective-permute-start.12 = (bf16[4,6,128,128]{3,2,1,0:T(8,128)(2,1)}, bf16[4,6,128,128]{3,2,1,0:T(8,128)(2,1)}, u32[]{:S(2)}, u32[]{:S(2)}) collective-permute-start(bf16[4,6,128,128]{3,2,1,0:T(8,128)(2,1)} %get-tuple-element.15.refs_1_.refs_14_), channel_id=1, source_target_pairs={{0,8},{8,16},{16,24},{24,32},{32,40},{40,48},{48,56},{56,0},{1,9},... | collective-permute-start | bytes 2359304 | tf_op jit(solution)/shard_map/ppermute | solution.py:23
  28.8 4.2 %copy-start.10 = (bf16[4,6,128,128]{3,2,1,0:T(8,128)(2,1)}, bf16[4,6,128,128]{3,2,1,0:T(8,128)(2,1)S(1)}, u32[]{:S(2)}) copy-start(bf16[4,6,128,128]{3,2,1,0:T(8,128)(2,1)S(1)} %collective-permute-done.6.refs_4_.refs_7_) | copy-start | bytes 2359300
  28.8 24.6 %collective-permute-start.13 = (bf16[4,6,128,128]{3,2,1,0:T(8,128)(2,1)}, bf16[4,6,128,128]{3,2,1,0:T(8,128)(2,1)}, u32[]{:S(2)}, u32[]{:S(2)}) collective-permute-start(bf16[4,6,128,128]{3,2,1,0:T(8,128)(2,1)} %get-tuple-element.16.refs_2_.refs_13_), channel_id=1, source_target_pairs={{0,56},{8,0},{16,8},{24,16},{32,24},{40,32},{48,40},{56,48},{1,57}... | collective-permute-start | bytes 2359304 | tf_op jit(solution)/shard_map/ppermute | solution.py:23
  33.0 0.8 copy-start.9
  33.7 47.8 %all-to-all-start.1 = ((bf16[8,5,2,128,128]{4,3,2,1,0:T(8,128)(2,1)}), bf16[8,5,2,128,128]{4,3,2,1,0:T(8,128)(2,1)S(1)}, u32[]{:S(2)}, u32[]{:S(2)}) async-start(bf16[8,5,2,128,128]{4,3,2,1,0:T(8,128)(2,1)} %get-tuple-element.14.refs_3_), calls=%async_computation.1 | async-start | bytes 5242880 | tf_op jit(solution)/shard_map/all_to_all | solution.py:249
  38.6 13.5 %collective-permute-start.10 = (bf16[8,3,2,32,128]{4,3,2,1,0:T(8,128)(2,1)}, bf16[8,3,2,32,128]{4,3,2,1,0:T(8,128)(2,1)}, u32[]{:S(2)}, u32[]{:S(2)}) collective-permute-start(bf16[8,3,2,32,128]{4,3,2,1,0:T(8,128)(2,1)} %shard_map.84.refs_8_), channel_id=1, source_target_pairs={{0,1},{1,2},{2,3},{3,0},{4,5},{5,6},{6,7},{7,4},{8,9},{9,10},{10,1... | collective-permute-start | bytes 1179656 | tf_op jit(solution)/shard_map/ppermute | solution.py:23
  39.9 13.5 %collective-permute-start.9 = (bf16[8,3,2,32,128]{4,3,2,1,0:T(8,128)(2,1)}, bf16[8,3,2,32,128]{4,3,2,1,0:T(8,128)(2,1)S(1)}, u32[]{:S(2)}, u32[]{:S(2)}) collective-permute-start(bf16[8,3,2,32,128]{4,3,2,1,0:T(8,128)(2,1)} %shard_map.84.refs_8_), channel_id=1, source_target_pairs={{0,3},{1,0},{2,1},{3,2},{4,7},{5,4},{6,5},{7,6},{8,11},{9,8},{10,9... | collective-permute-start | bytes 1179656 | tf_op jit(solution)/shard_map/ppermute | solution.py:23
  49.8 7.1 %collective-permute-start.5 = (bf16[4,6,128,128]{3,2,1,0:T(8,128)(2,1)}, bf16[4,6,128,128]{3,2,1,0:T(8,128)(2,1)}, u32[]{:S(2)}, u32[]{:S(2)}) collective-permute-start(bf16[4,6,128,128]{3,2,1,0:T(8,128)(2,1)} %collective-permute-done.4.refs_4_), channel_id=1, source_target_pairs={{0,4},{4,0},{1,5},{5,1},{2,6},{6,2},{3,7},{7,3},{8,12},{12,8},{9,1... | collective-permute-start | bytes 2359304 | tf_op jit(solution)/shard_map/ppermute | solution.py:23
  52.1 12.4 %collective-permute-start.11 = (bf16[8,3,2,32,128]{4,3,2,1,0:T(8,128)(2,1)}, bf16[8,3,2,32,128]{4,3,2,1,0:T(8,128)(2,1)}, u32[]{:S(2)}, u32[]{:S(2)}) collective-permute-start(bf16[8,3,2,32,128]{4,3,2,1,0:T(8,128)(2,1)} %collective-permute-done.10.refs_3_.refs_11_), channel_id=1, source_target_pairs={{0,1},{1,2},{2,3},{3,0},{4,5},{5,6},{6,7},{7,4},{8,9},{9,10},{10,1... | collective-permute-start | bytes 1179656 | tf_op jit(solution)/shard_map/ppermute | solution.py:23
  53.5 0.8 copy-start.16
  54.2 20.3 %collective-permute-start.14 = (bf16[4,6,128,128]{3,2,1,0:T(8,128)(2,1)}, bf16[4,6,128,128]{3,2,1,0:T(8,128)(2,1)S(1)}, u32[]{:S(2)}, u32[]{:S(2)}) collective-permute-start(bf16[4,6,128,128]{3,2,1,0:T(8,128)(2,1)} %get-tuple-element.17.refs_15_.refs_10_), channel_id=1, source_target_pairs={{0,8},{8,16},{16,24},{24,32},{32,40},{40,48},{48,56},{56,0},{1,9},... | collective-permute-start | bytes 2359304 | tf_op jit(solution)/shard_map/ppermute | solution.py:23
  54.2 20.3 %collective-permute-start.15 = (bf16[4,6,128,128]{3,2,1,0:T(8,128)(2,1)}, bf16[4,6,128,128]{3,2,1,0:T(8,128)(2,1)}, u32[]{:S(2)}, u32[]{:S(2)}) collective-permute-start(bf16[4,6,128,128]{3,2,1,0:T(8,128)(2,1)} %get-tuple-element.18.refs_16_.refs_9_), channel_id=1, source_target_pairs={{0,56},{8,0},{16,8},{24,16},{32,24},{40,32},{48,40},{56,48},{1,57}... | collective-permute-start | bytes 2359304 | tf_op jit(solution)/shard_map/ppermute | solution.py:23
  74.5 0.9 copy-start.13
  75.4 4.9 %copy-start.8 = (bf16[4,8,3,2,32,128]{5,4,3,2,1,0:T(8,128)(2,1)S(1)}, bf16[4,8,3,2,32,128]{5,4,3,2,1,0:T(8,128)(2,1)}, u32[]{:S(2)}) copy-start(bf16[4,8,3,2,32,128]{5,4,3,2,1,0:T(8,128)(2,1)} %shard_map.86.refs_2_.refs_15_) | copy-start | bytes 4718596
  77.5 11.5 %collective-permute-start.16 = (bf16[2,6,128,128]{3,2,1,0:T(8,128)(2,1)S(1)}, bf16[2,6,128,128]{3,2,1,0:T(8,128)(2,1)}, u32[]{:S(2)}, u32[]{:S(2)}) collective-permute-start(bf16[2,6,128,128]{3,2,1,0:T(8,128)(2,1)S(1)} %slice.6), channel_id=1, source_target_pairs={{0,8},{8,16},{16,24},{24,32},{32,40},{40,48},{48,56},{56,0},{1,9},... | collective-permute-start | bytes 1179656 | tf_op jit(solution)/shard_map/ppermute | solution.py:23
  77.6 11.4 %collective-permute-start.17 = (bf16[2,6,128,128]{3,2,1,0:T(8,128)(2,1)S(1)}, bf16[2,6,128,128]{3,2,1,0:T(8,128)(2,1)}, u32[]{:S(2)}, u32[]{:S(2)}) collective-permute-start(bf16[2,6,128,128]{3,2,1,0:T(8,128)(2,1)S(1)} %slice.7), channel_id=1, source_target_pairs={{0,56},{8,0},{16,8},{24,16},{32,24},{40,32},{48,40},{56,48},{1,57}... | collective-permute-start | bytes 1179656 | tf_op jit(solution)/shard_map/ppermute | solution.py:23
  81.5 1.5 copy-start.7
  83.0 28.1 %all-to-all-start.2 = ((bf16[32,3,2,32,128]{4,3,2,1,0:T(8,128)(2,1)}), bf16[32,3,2,32,128]{4,3,2,1,0:T(8,128)(2,1)S(1)}, u32[]{:S(2)}, u32[]{:S(2)}) async-start(bf16[32,3,2,32,128]{4,3,2,1,0:T(8,128)(2,1)} %bitcast.13), calls=%async_computation.2 | async-start | bytes 3145728 | tf_op jit(solution)/shard_map/all_to_all | solution.py:273
  111.1 40.1 %copy-start.2 = (s32[384]{0:T(512)S(1)}, s32[384]{0:T(512)}, u32[]{:S(2)}) copy-start(s32[384]{0:T(512)} %right_dims.3) | copy-start | bytes 4612
  111.1 40.1 %copy-start.4 = (s32[4]{0:T(128)S(1)}, s32[4]{0:T(128)}, u32[]{:S(2)}) copy-start(s32[4]{0:T(128)} %copy-done.3) | copy-start | bytes 52
  111.1 40.1 %copy-start.6 = (s32[8]{0:T(128)S(1)}, s32[8]{0:T(128)}, u32[]{:S(2)}) copy-start(s32[8]{0:T(128)} %constant.95.clone.place) | copy-start | bytes 100

commit v3 on v2

--- a/solution.py
+++ b/solution.py
@@ -149,7 +149,7 @@
     for far in range(4):
         quarter = lax.rem(y + far, 4) if relative else far
         row = pl.multiple_of(quarter * rows, rows)
-        copy(total.at[:, :, :, pl.ds(row, rows)], out.at[far])
+        copy(total.at[:, :, :, pl.ds(row, rows)], out.at[:, far])
     for ready in copies:
         ready.wait()
 
@@ -162,7 +162,7 @@
     flat = [part for parts in rights for part in parts]
     return pl.pallas_call(
         functools.partial(chunk_kernel, first, count, begin, quarters, halves, relative),
-        out_shape=jax.ShapeDtypeStruct((4, sources, count, CAP, rows, size), jnp.bfloat16),
+        out_shape=jax.ShapeDtypeStruct((sources, 4, count, CAP, rows, size), jnp.bfloat16),
         in_specs=[SMEM] * 3 + [ANY] * (8 + quarters + len(flat) + len(after)),
         out_specs=ANY,
         scratch_shapes=[
@@ -199,15 +199,15 @@
 
             @pl.when((step >= start) & (step < start + count))
             def _(part=part, planes=planes, start=start):
-                whole = part[lane, step - start, rank].astype(jnp.float32)
+                whole = part[lane * planes, step - start, rank].astype(jnp.float32)
                 for plane in range(1, planes):
-                    whole += part[plane * 8 + lane, step - start, rank].astype(jnp.float32)
+                    whole += part[lane * planes + plane, step - start, rank].astype(jnp.float32)
                 out[tile] = jnp.where(keep, whole, 0.0).astype(out.dtype)
 
             start += count
         return 0
 
-    lax.fori_loop(0, tiles, one_tile, 0)
+    lax.fori_loop(0, tiles, one_tile, 0, unroll=4)
 
 
 def on_device(wavefunction, left_env, right_env, left_dims, right_dims, partner):
@@ -270,7 +270,7 @@
 
     def straight_back(partial):
         partial = partial.reshape(ny * lanes, *partial.shape[2:])
-        return lax.all_to_all(partial, ("y", "x", "k"), 0, 0, tiled=True)
+        return lax.all_to_all(partial, ("x", "k", "y"), 0, 0, tiled=True)
 
     rights = [[right_env], *[[two_way] for two_way in (one[1], one[0])]]
     first = chunk(0, EARLY, early, [*two])

time: 157 us -> 155 us (0.987)
  no operation moved by 1% of the time
where the time goes in v3:
time: 155 us
  starting transfers between devices  41.1 us (27%)
  blocking collectives  39 us (25%)
  Pallas kernels  31.2 us (20%)
  waiting for transfers between devices  28.2 us (18%)
  local copies, waits for them, and re-layouts  13.7 us (9%)
    all_to_all x1, blocking collectives, straight_back(): return lax.all_to_all(partial, ('x', 'k', 'y'), 0, 0, tiled=True)  39 us
    ppermute x18, starting transfers between devices, shift(): lax.ppermute(array, axis, [(i, (i + by) % count) for i in range(count)])  26.8 us
    pallas_call x2, Pallas kernels, compute_chunk(): pl.pallas_call(functools.partial(chunk_kernel, first, count, begin, quart...  20.2 us
    ppermute x18, waiting for transfers between devices, shift(): lax.ppermute(array, axis, [(i, (i + by) % count) for i in range(count)])  16.9 us
    all_to_all x1, waiting for transfers between devices, straight_back(): return lax.all_to_all(partial, ('x', 'k', 'y'), 0, 0, tiled=True)  9.81 us
    unnamed x36, local copies, waits for them, and re-layouts  9.43 us
    all_to_all x1, starting transfers between devices, straight_back(): return lax.all_to_all(partial, ('x', 'k', 'y'), 0, 0, tiled=True)  6.03 us
    pallas_call x1, Pallas kernels, on_device(): pl.pallas_call(send_kernel, out_shape=[jax.ShapeDtypeStruct((lanes, EARLY...  5.87 us
  transfers between devices with their start and end apart: 21, of which 5 were waited for; matrix products, arithmetic and copies ran while one was open for 4% of the time, Pallas kernels for 17%

profile of v3, /device:TPU:1, one launch (start us, length us, event | category | flops | bytes accessed | tf_op | source)
XLA Modules:
  0.0 154.7 jit_solution(5910973487733850216)
XLA Ops:
  0.0 2.0 %collective-permute-start.3 = (bf16[4,6,128,128]{3,2,1,0:T(8,128)(2,1)}, bf16[4,6,128,128]{3,2,1,0:T(8,128)(2,1)}, u32[]{:S(2)}, u32[]{:S(2)}) collective-permute-start(bf16[4,6,128,128]{3,2,1,0:T(8,128)(2,1)} %refs_0_.3), channel_id=1, source_target_pairs={{0,64},{64,128},{128,192},{192,0},{1,65},{65,129},{129,193},{193,1... | collective-permute-start | bytes 2359304 | tf_op jit(solution)/shard_map/ppermute | solution.py:23
  2.0 1.6 %collective-permute-start.7 = (bf16[4,6,128,128]{3,2,1,0:T(8,128)(2,1)}, bf16[4,6,128,128]{3,2,1,0:T(8,128)(2,1)S(1)}, u32[]{:S(2)}, u32[]{:S(2)}) collective-permute-start(bf16[4,6,128,128]{3,2,1,0:T(8,128)(2,1)} %refs_12_.1), channel_id=1, source_target_pairs={{0,8},{8,16},{16,24},{24,32},{32,40},{40,48},{48,56},{56,0},{1,9},... | collective-permute-start | bytes 2359304 | tf_op jit(solution)/shard_map/ppermute | solution.py:23
  3.7 1.5 collective-permute-start.1
  5.1 3.9 %collective-permute-start.8 = (bf16[4,6,128,128]{3,2,1,0:T(8,128)(2,1)}, bf16[4,6,128,128]{3,2,1,0:T(8,128)(2,1)S(1)}, u32[]{:S(2)}, u32[]{:S(2)}) collective-permute-start(bf16[4,6,128,128]{3,2,1,0:T(8,128)(2,1)} %refs_12_.1), channel_id=1, source_target_pairs={{0,56},{8,0},{16,8},{24,16},{32,24},{40,32},{48,40},{56,48},{1,57}... | collective-permute-start | bytes 2359304 | tf_op jit(solution)/shard_map/ppermute | solution.py:23
  9.1 1.5 collective-permute-start
  10.6 0.8 dynamic_slice.11.left_dims
  11.4 0.8 constant_dynamic-slice_fusion
  12.2 0.1 copy.22
  12.2 0.1 reshape.96.partner
  12.3 0.1 pad_add_fusion.1.spot
  12.4 1.9 %copy-done = bf16[6,16,128,128]{3,2,1,0:T(8,128)(2,1)S(1)} copy-done((bf16[6,16,128,128]{3,2,1,0:T(8,128)(2,1)S(1)}, bf16[6,16,128,128]{3,2,1,0:T(8,128)(2,1)}, u32[]{:S(2)}) %copy-start) | copy-done | bytes 3145752
  14.3 0.7 copy-done.1
  15.0 0.7 copy-done.5
  15.6 5.9 %shard_map.82 = (bf16[8,3,2,32,128]{4,3,2,1,0:T(8,128)(2,1)}, bf16[8,5,2,128,128]{4,3,2,1,0:T(8,128)(2,1)}) custom-call(s32[4]{0:T(128)S(1)} %pad_add_fusion.1.spot, s32[8]{0:T(128)S(1)} %copy-done.5, s32[96]{0:T(128)S(1)} %reshape.96.partner, s32[6]{0:T(128)S(1)} %dynamic_slice.11.left_dims, s32[384]{0:T(512)S(1)} %copy-done.1, ...), custom_call_target="tpu_custom_call" | custom-call | tf_op jit(solution)/shard_map/pallas_call | solution.py:232
  21.5 3.4 %all-to-all-start = ((bf16[8,3,2,32,128]{4,3,2,1,0:T(8,128)(2,1)}), bf16[8,3,2,32,128]{4,3,2,1,0:T(8,128)(2,1)S(1)}, u32[]{:S(2)}, u32[]{:S(2)}) async-start(bf16[8,3,2,32,128]{4,3,2,1,0:T(8,128)(2,1)} %get-tuple-element.13.refs_2_), calls=%async_computation | async-start | bytes 786432 | tf_op jit(solution)/shard_map/all_to_all | solution.py:248
  24.9 0.1 copy.23
  25.0 0.1 reshape.97
  25.2 0.0 collective-permute-done.3.refs_6_
  25.2 0.1 collective-permute-start.6
  25.4 0.0 collective-permute-done.7.refs_0_
  25.4 1.7 %collective-permute-start.4 = (bf16[4,6,128,128]{3,2,1,0:T(8,128)(2,1)}, bf16[4,6,128,128]{3,2,1,0:T(8,128)(2,1)}, u32[]{:S(2)}, u32[]{:S(2)}) collective-permute-start(bf16[4,6,128,128]{3,2,1,0:T(8,128)(2,1)} %collective-permute-done.3.refs_6_), channel_id=1, source_target_pairs={{0,64},{64,128},{128,192},{192,0},{1,65},{65,129},{129,193},{193,1... | collective-permute-start | bytes 2359304 | tf_op jit(solution)/shard_map/ppermute | solution.py:23
  27.1 0.0 collective-permute-done.1.refs_2_
  27.1 0.7 collective-permute-start.2
  27.8 0.0 collective-permute-done.8.refs_1_
  27.8 0.9 copy-done.12
  28.8 0.0 copy-start.10
  28.8 2.7 %collective-permute-start.13 = (bf16[4,6,128,128]{3,2,1,0:T(8,128)(2,1)}, bf16[4,6,128,128]{3,2,1,0:T(8,128)(2,1)}, u32[]{:S(2)}, u32[]{:S(2)}) collective-permute-start(bf16[4,6,128,128]{3,2,1,0:T(8,128)(2,1)} %get-tuple-element.16.refs_2_.refs_13_), channel_id=1, source_target_pairs={{0,56},{8,0},{16,8},{24,16},{32,24},{40,32},{48,40},{56,48},{1,57}... | collective-permute-start | bytes 2359304 | tf_op jit(solution)/shard_map/ppermute | solution.py:23
  31.5 1.5 all-to-all-done.refs_0_
  33.0 0.8 copy-done.9
  33.7 4.9 %all-to-all-start.1 = ((bf16[8,5,2,128,128]{4,3,2,1,0:T(8,128)(2,1)}), bf16[8,5,2,128,128]{4,3,2,1,0:T(8,128)(2,1)S(1)}, u32[]{:S(2)}, u32[]{:S(2)}) async-start(bf16[8,5,2,128,128]{4,3,2,1,0:T(8,128)(2,1)} %get-tuple-element.14.refs_3_), calls=%async_computation.1 | async-start | bytes 5242880 | tf_op jit(solution)/shard_map/all_to_all | solution.py:249
  38.6 0.0 collective-permute-done.2.refs_3_
  38.6 1.3 collective-permute-start.10
  39.9 0.0 collective-permute-done.refs_4_.refs_1_
  39.9 1.5 collective-permute-start.9
  41.4 0.4 fusion
  41.9 7.9 %collective-permute-done.4.refs_4_ = bf16[4,6,128,128]{3,2,1,0:T(8,128)(2,1)} collective-permute-done((bf16[4,6,128,128]{3,2,1,0:T(8,128)(2,1)}, bf16[4,6,128,128]{3,2,1,0:T(8,128)(2,1)}, u32[]{:S(2)}, u32[]{:S(2)}) %collective-permute-start.4) | collective-permute-done | bytes 786464 | tf_op jit(solution)/shard_map/ppermute | solution.py:23
  49.8 1.5 collective-permute-start.5
  51.2 0.1 copy.24
  51.4 0.1 reshape.98
  51.5 0.6 fusion.7
  52.1 1.3 collective-permute-start.11
  53.4 0.0 collective-permute-done.12.refs_0_
  53.4 0.0 collective-permute-done.13.refs_1_
  53.4 0.0 collective-permute-done.9.refs_2_.refs_9_
  53.4 0.7 copy-done.16
  54.2 2.7 %collective-permute-start.15 = (bf16[4,6,128,128]{3,2,1,0:T(8,128)(2,1)}, bf16[4,6,128,128]{3,2,1,0:T(8,128)(2,1)}, u32[]{:S(2)}, u32[]{:S(2)}) collective-permute-start(bf16[4,6,128,128]{3,2,1,0:T(8,128)(2,1)} %get-tuple-element.18.refs_16_.refs_9_), channel_id=1, source_target_pairs={{0,56},{8,0},{16,8},{24,16},{32,24},{40,32},{48,40},{56,48},{1,57}... | collective-permute-start | bytes 2359304 | tf_op jit(solution)/shard_map/ppermute | solution.py:23
  56.9 0.0 collective-permute-done.5.refs_5_
  56.9 7.7 %collective-permute-done.11.refs_10_ = bf16[8,3,2,32,128]{4,3,2,1,0:T(8,128)(2,1)} collective-permute-done((bf16[8,3,2,32,128]{4,3,2,1,0:T(8,128)(2,1)}, bf16[8,3,2,32,128]{4,3,2,1,0:T(8,128)(2,1)}, u32[]{:S(2)}, u32[]{:S(2)}) %collective-permute-start.11) | collective-permute-done | bytes 393248 | tf_op jit(solution)/shard_map/ppermute | solution.py:23
  64.5 8.6 %shard_map.86.refs_2_.refs_15_ = bf16[8,4,3,2,32,128]{5,4,3,2,1,0:T(8,128)(2,1)} custom-call(s32[4]{0:T(128)} %copy-done.3, s32[128]{0:T(128)} %get-tuple-element.28.left_at, s32[128]{0:T(128)} %get-tuple-element.27.right_at, bf16[4,6,128,128]{3,2,1,0:T(8,128)(2,1)} %refs_0_.3, bf16[4,6,128,128]{3,2,1,0:T(8,128)(2,1)} %collective-permute-done.refs_4_.refs_1_, ...), custom_call_target="tpu_custom_call" | custom-call | flops 9663676416 | bytes 3145728 | tf_op jit(solution)/shard_map/pallas_call | solution.py:163
  73.2 1.3 collective-permute-done.14.refs_0_
  74.5 0.0 collective-permute-done.15.refs_1_
  74.5 0.9 copy-done.13
  75.4 1.1 slice.7
  76.5 1.0 slice.6
  77.5 0.1 collective-permute-start.16
  77.6 2.7 %collective-permute-start.17 = (bf16[2,6,128,128]{3,2,1,0:T(8,128)(2,1)S(1)}, bf16[2,6,128,128]{3,2,1,0:T(8,128)(2,1)}, u32[]{:S(2)}, u32[]{:S(2)}) collective-permute-start(bf16[2,6,128,128]{3,2,1,0:T(8,128)(2,1)S(1)} %slice.7), channel_id=1, source_target_pairs={{0,56},{8,0},{16,8},{24,16},{32,24},{40,32},{48,40},{56,48},{1,57}... | collective-permute-start | bytes 1179656 | tf_op jit(solution)/shard_map/ppermute | solution.py:23
  80.3 1.2 copy.30.refs_0_
  81.5 1.5 copy-done.7
  83.0 6.0 %all-to-all-start.2 = ((bf16[32,3,2,32,128]{4,3,2,1,0:T(8,128)(2,1)}), bf16[32,3,2,32,128]{4,3,2,1,0:T(8,128)(2,1)S(1)}, u32[]{:S(2)}, u32[]{:S(2)}) async-start(bf16[32,3,2,32,128]{4,3,2,1,0:T(8,128)(2,1)} %bitcast.13), calls=%async_computation.2 | async-start | bytes 3145728 | tf_op jit(solution)/shard_map/all_to_all | solution.py:273
  89.0 0.0 collective-permute-done.16.refs_13_
  89.1 11.6 %shard_map.89 = bf16[8,4,5,2,32,128]{5,4,3,2,1,0:T(8,128)(2,1)} custom-call(s32[4]{0:T(128)} %copy-done.3, s32[128]{0:T(128)} %get-tuple-element.28.left_at, s32[128]{0:T(128)} %get-tuple-element.27.right_at, bf16[4,6,128,128]{3,2,1,0:T(8,128)(2,1)} %refs_0_.3, bf16[4,6,128,128]{3,2,1,0:T(8,128)(2,1)} %collective-permute-done.refs_4_.refs_1_, ...), custom_call_target="tpu_custom_call" | custom-call | flops 16106127360 | bytes 5242880 | tf_op jit(solution)/shard_map/pallas_call | solution.py:163
  100.7 9.8 %all-to-all-done.2.refs_0_ = bf16[32,3,2,32,128]{4,3,2,1,0:T(8,128)(2,1)S(1)} async-done(((bf16[32,3,2,32,128]{4,3,2,1,0:T(8,128)(2,1)}), bf16[32,3,2,32,128]{4,3,2,1,0:T(8,128)(2,1)S(1)}, u32[]{:S(2)}, u32[]{:S(2)}) %all-to-all-start.2) | async-done | bytes 1572896 | tf_op jit(solution)/shard_map/all_to_all | solution.py:273
  110.5 39.0 %all_to_all.20.refs_1_ = bf16[32,5,2,32,128]{4,3,2,1,0:T(8,128)(2,1)S(1)} all-to-all(bf16[32,5,2,32,128]{4,3,2,1,0:T(8,128)(2,1)} %bitcast.14), channel_id=1, replica_groups=mesh['x'=4,'z'=8,'k'=2,'y'=4] {'x','k','y'}, dimensions={0} | all-to-all | bytes 5242880 | tf_op jit(solution)/shard_map/all_to_all | solution.py:273
  149.6 5.1 %shard_map.90 = bf16[96,32,128]{2,1,0:T(8,128)(2,1)} custom-call(s32[4]{0:T(128)S(1)} %copy-done.4, s32[8]{0:T(128)S(1)} %copy-done.6, s32[96]{0:T(128)S(1)} %reshape.96.partner, s32[6]{0:T(128)S(1)} %dynamic_slice.11.left_dims, s32[384]{0:T(512)S(1)} %copy-done.2, bf16[32,3,2,32,128]{4,3,2,1,0:T(8,128)(2,1)S(1)} %all-to-all-done.2.refs_0_, ...), custom_call_target="tpu_custom_call" | custom-call | tf_op jit(solution)/shard_map/pallas_call | solution.py:285
  (43 shorter events, 0.1 us)
Async XLA Ops:
  0.0 25.4 %copy-start.15 = (s32[8]{0:T(128)S(1)}, s32[8]{0:T(128)}, u32[]{:S(2)}) copy-start(s32[8]{0:T(128)} %constant.94.clone) | copy-start | bytes 100
  0.0 24.9 %copy-start.14 = (s32[384,16]{0,1:T(8,128)S(1)}, s32[384,16]{0,1:T(8,128)}, u32[]{:S(2)}) copy-start(s32[384,16]{0,1:T(8,128)} %param.13) | copy-start | bytes 73732
  0.0 25.2 %collective-permute-start.3 = (bf16[4,6,128,128]{3,2,1,0:T(8,128)(2,1)}, bf16[4,6,128,128]{3,2,1,0:T(8,128)(2,1)}, u32[]{:S(2)}, u32[]{:S(2)}) collective-permute-start(bf16[4,6,128,128]{3,2,1,0:T(8,128)(2,1)} %refs_0_.3), channel_id=1, source_target_pairs={{0,64},{64,128},{128,192},{192,0},{1,65},{65,129},{129,193},{193,1... | collective-permute-start | bytes 2359304 | tf_op jit(solution)/shard_map/ppermute | solution.py:23
  2.0 23.3 %collective-permute-start.7 = (bf16[4,6,128,128]{3,2,1,0:T(8,128)(2,1)}, bf16[4,6,128,128]{3,2,1,0:T(8,128)(2,1)S(1)}, u32[]{:S(2)}, u32[]{:S(2)}) collective-permute-start(bf16[4,6,128,128]{3,2,1,0:T(8,128)(2,1)} %refs_12_.1), channel_id=1, source_target_pairs={{0,8},{8,16},{16,24},{24,32},{32,40},{40,48},{48,56},{56,0},{1,9},... | collective-permute-start | bytes 2359304 | tf_op jit(solution)/shard_map/ppermute | solution.py:23
  3.7 23.4 %collective-permute-start.1 = (bf16[4,6,128,128]{3,2,1,0:T(8,128)(2,1)}, bf16[4,6,128,128]{3,2,1,0:T(8,128)(2,1)}, u32[]{:S(2)}, u32[]{:S(2)}) collective-permute-start(bf16[4,6,128,128]{3,2,1,0:T(8,128)(2,1)} %refs_0_.3), channel_id=1, source_target_pairs={{0,192},{64,0},{128,64},{192,128},{1,193},{65,1},{129,65},{193,129... | collective-permute-start | bytes 2359304 | tf_op jit(solution)/shard_map/ppermute | solution.py:23
  5.1 22.7 %collective-permute-start.8 = (bf16[4,6,128,128]{3,2,1,0:T(8,128)(2,1)}, bf16[4,6,128,128]{3,2,1,0:T(8,128)(2,1)S(1)}, u32[]{:S(2)}, u32[]{:S(2)}) collective-permute-start(bf16[4,6,128,128]{3,2,1,0:T(8,128)(2,1)} %refs_12_.1), channel_id=1, source_target_pairs={{0,56},{8,0},{16,8},{24,16},{32,24},{40,32},{48,40},{56,48},{1,57}... | collective-permute-start | bytes 2359304 | tf_op jit(solution)/shard_map/ppermute | solution.py:23
  9.1 30.8 %collective-permute-start = (bf16[4,6,128,128]{3,2,1,0:T(8,128)(2,1)}, bf16[4,6,128,128]{3,2,1,0:T(8,128)(2,1)}, u32[]{:S(2)}, u32[]{:S(2)}) collective-permute-start(bf16[4,6,128,128]{3,2,1,0:T(8,128)(2,1)} %refs_0_.3), channel_id=1, source_target_pairs={{0,4},{4,0},{1,5},{5,1},{2,6},{6,2},{3,7},{7,3},{8,12},{12,8},{9,1... | collective-permute-start | bytes 2359304 | tf_op jit(solution)/shard_map/ppermute | solution.py:23
  12.4 16.4 %copy-start.3 = (s32[4]{0:T(128)}, s32[4]{0:T(128)S(1)}, u32[]{:S(2)}) copy-start(s32[4]{0:T(128)S(1)} %pad_add_fusion.1.spot) | copy-start | bytes 52
  12.4 1.9 %copy-start = (bf16[6,16,128,128]{3,2,1,0:T(8,128)(2,1)S(1)}, bf16[6,16,128,128]{3,2,1,0:T(8,128)(2,1)}, u32[]{:S(2)}) copy-start(bf16[6,16,128,128]{3,2,1,0:T(8,128)(2,1)} %param.8) | copy-start | bytes 9437188
  14.3 0.7 copy-start.1
  15.0 0.7 copy-start.5
  21.5 11.5 %all-to-all-start = ((bf16[8,3,2,32,128]{4,3,2,1,0:T(8,128)(2,1)}), bf16[8,3,2,32,128]{4,3,2,1,0:T(8,128)(2,1)S(1)}, u32[]{:S(2)}, u32[]{:S(2)}) async-start(bf16[8,3,2,32,128]{4,3,2,1,0:T(8,128)(2,1)} %get-tuple-element.13.refs_2_), calls=%async_computation | async-start | bytes 786432 | tf_op jit(solution)/shard_map/all_to_all | solution.py:248
  25.2 3.5 %collective-permute-start.6 = (bf16[4,6,128,128]{3,2,1,0:T(8,128)(2,1)}, bf16[4,6,128,128]{3,2,1,0:T(8,128)(2,1)S(1)}, u32[]{:S(2)}, u32[]{:S(2)}) collective-permute-start(bf16[4,6,128,128]{3,2,1,0:T(8,128)(2,1)} %collective-permute-done.3.refs_6_), channel_id=1, source_target_pairs={{0,4},{4,0},{1,5},{5,1},{2,6},{6,2},{3,7},{7,3},{8,12},{12,8},{9,1... | collective-permute-start | bytes 2359304 | tf_op jit(solution)/shard_map/ppermute | solution.py:23
  25.4 2.4 %copy-start.11 = (bf16[4,6,128,128]{3,2,1,0:T(8,128)(2,1)}, bf16[4,6,128,128]{3,2,1,0:T(8,128)(2,1)S(1)}, u32[]{:S(2)}) copy-start(bf16[4,6,128,128]{3,2,1,0:T(8,128)(2,1)S(1)} %collective-permute-done.7.refs_0_) | copy-start | bytes 2359300
  25.4 24.4 %collective-permute-start.4 = (bf16[4,6,128,128]{3,2,1,0:T(8,128)(2,1)}, bf16[4,6,128,128]{3,2,1,0:T(8,128)(2,1)}, u32[]{:S(2)}, u32[]{:S(2)}) collective-permute-start(bf16[4,6,128,128]{3,2,1,0:T(8,128)(2,1)} %collective-permute-done.3.refs_6_), channel_id=1, source_target_pairs={{0,64},{64,128},{128,192},{192,0},{1,65},{65,129},{129,193},{193,1... | collective-permute-start | bytes 2359304 | tf_op jit(solution)/shard_map/ppermute | solution.py:23
  27.1 11.5 %collective-permute-start.2 = (bf16[4,6,128,128]{3,2,1,0:T(8,128)(2,1)}, bf16[4,6,128,128]{3,2,1,0:T(8,128)(2,1)}, u32[]{:S(2)}, u32[]{:S(2)}) collective-permute-start(bf16[4,6,128,128]{3,2,1,0:T(8,128)(2,1)} %collective-permute-done.1.refs_2_), channel_id=1, source_target_pairs={{0,4},{4,0},{1,5},{5,1},{2,6},{6,2},{3,7},{7,3},{8,12},{12,8},{9,1... | collective-permute-start | bytes 2359304 | tf_op jit(solution)/shard_map/ppermute | solution.py:23
  27.8 0.9 copy-start.12
  28.8 24.7 %collective-permute-start.12 = (bf16[4,6,128,128]{3,2,1,0:T(8,128)(2,1)}, bf16[4,6,128,128]{3,2,1,0:T(8,128)(2,1)}, u32[]{:S(2)}, u32[]{:S(2)}) collective-permute-start(bf16[4,6,128,128]{3,2,1,0:T(8,128)(2,1)} %get-tuple-element.15.refs_1_.refs_14_), channel_id=1, source_target_pairs={{0,8},{8,16},{16,24},{24,32},{32,40},{40,48},{48,56},{56,0},{1,9},... | collective-permute-start | bytes 2359304 | tf_op jit(solution)/shard_map/ppermute | solution.py:23
  28.8 4.2 %copy-start.10 = (bf16[4,6,128,128]{3,2,1,0:T(8,128)(2,1)}, bf16[4,6,128,128]{3,2,1,0:T(8,128)(2,1)S(1)}, u32[]{:S(2)}) copy-start(bf16[4,6,128,128]{3,2,1,0:T(8,128)(2,1)S(1)} %collective-permute-done.6.refs_4_.refs_7_) | copy-start | bytes 2359300
  28.8 24.6 %collective-permute-start.13 = (bf16[4,6,128,128]{3,2,1,0:T(8,128)(2,1)}, bf16[4,6,128,128]{3,2,1,0:T(8,128)(2,1)}, u32[]{:S(2)}, u32[]{:S(2)}) collective-permute-start(bf16[4,6,128,128]{3,2,1,0:T(8,128)(2,1)} %get-tuple-element.16.refs_2_.refs_13_), channel_id=1, source_target_pairs={{0,56},{8,0},{16,8},{24,16},{32,24},{40,32},{48,40},{56,48},{1,57}... | collective-permute-start | bytes 2359304 | tf_op jit(solution)/shard_map/ppermute | solution.py:23
  33.0 0.8 copy-start.9
  33.7 47.8 %all-to-all-start.1 = ((bf16[8,5,2,128,128]{4,3,2,1,0:T(8,128)(2,1)}), bf16[8,5,2,128,128]{4,3,2,1,0:T(8,128)(2,1)S(1)}, u32[]{:S(2)}, u32[]{:S(2)}) async-start(bf16[8,5,2,128,128]{4,3,2,1,0:T(8,128)(2,1)} %get-tuple-element.14.refs_3_), calls=%async_computation.1 | async-start | bytes 5242880 | tf_op jit(solution)/shard_map/all_to_all | solution.py:249
  38.6 13.5 %collective-permute-start.10 = (bf16[8,3,2,32,128]{4,3,2,1,0:T(8,128)(2,1)}, bf16[8,3,2,32,128]{4,3,2,1,0:T(8,128)(2,1)}, u32[]{:S(2)}, u32[]{:S(2)}) collective-permute-start(bf16[8,3,2,32,128]{4,3,2,1,0:T(8,128)(2,1)} %shard_map.84.refs_8_), channel_id=1, source_target_pairs={{0,1},{1,2},{2,3},{3,0},{4,5},{5,6},{6,7},{7,4},{8,9},{9,10},{10,1... | collective-permute-start | bytes 1179656 | tf_op jit(solution)/shard_map/ppermute | solution.py:23
  39.9 13.5 %collective-permute-start.9 = (bf16[8,3,2,32,128]{4,3,2,1,0:T(8,128)(2,1)}, bf16[8,3,2,32,128]{4,3,2,1,0:T(8,128)(2,1)S(1)}, u32[]{:S(2)}, u32[]{:S(2)}) collective-permute-start(bf16[8,3,2,32,128]{4,3,2,1,0:T(8,128)(2,1)} %shard_map.84.refs_8_), channel_id=1, source_target_pairs={{0,3},{1,0},{2,1},{3,2},{4,7},{5,4},{6,5},{7,6},{8,11},{9,8},{10,9... | collective-permute-start | bytes 1179656 | tf_op jit(solution)/shard_map/ppermute | solution.py:23
  49.8 7.1 %collective-permute-start.5 = (bf16[4,6,128,128]{3,2,1,0:T(8,128)(2,1)}, bf16[4,6,128,128]{3,2,1,0:T(8,128)(2,1)}, u32[]{:S(2)}, u32[]{:S(2)}) collective-permute-start(bf16[4,6,128,128]{3,2,1,0:T(8,128)(2,1)} %collective-permute-done.4.refs_4_), channel_id=1, source_target_pairs={{0,4},{4,0},{1,5},{5,1},{2,6},{6,2},{3,7},{7,3},{8,12},{12,8},{9,1... | collective-permute-start | bytes 2359304 | tf_op jit(solution)/shard_map/ppermute | solution.py:23
  52.1 12.4 %collective-permute-start.11 = (bf16[8,3,2,32,128]{4,3,2,1,0:T(8,128)(2,1)}, bf16[8,3,2,32,128]{4,3,2,1,0:T(8,128)(2,1)}, u32[]{:S(2)}, u32[]{:S(2)}) collective-permute-start(bf16[8,3,2,32,128]{4,3,2,1,0:T(8,128)(2,1)} %collective-permute-done.10.refs_3_.refs_11_), channel_id=1, source_target_pairs={{0,1},{1,2},{2,3},{3,0},{4,5},{5,6},{6,7},{7,4},{8,9},{9,10},{10,1... | collective-permute-start | bytes 1179656 | tf_op jit(solution)/shard_map/ppermute | solution.py:23
  53.4 0.8 copy-start.16
  54.2 20.3 %collective-permute-start.14 = (bf16[4,6,128,128]{3,2,1,0:T(8,128)(2,1)}, bf16[4,6,128,128]{3,2,1,0:T(8,128)(2,1)S(1)}, u32[]{:S(2)}, u32[]{:S(2)}) collective-permute-start(bf16[4,6,128,128]{3,2,1,0:T(8,128)(2,1)} %get-tuple-element.17.refs_15_.refs_10_), channel_id=1, source_target_pairs={{0,8},{8,16},{16,24},{24,32},{32,40},{40,48},{48,56},{56,0},{1,9},... | collective-permute-start | bytes 2359304 | tf_op jit(solution)/shard_map/ppermute | solution.py:23
  54.2 20.3 %collective-permute-start.15 = (bf16[4,6,128,128]{3,2,1,0:T(8,128)(2,1)}, bf16[4,6,128,128]{3,2,1,0:T(8,128)(2,1)}, u32[]{:S(2)}, u32[]{:S(2)}) collective-permute-start(bf16[4,6,128,128]{3,2,1,0:T(8,128)(2,1)} %get-tuple-element.18.refs_16_.refs_9_), channel_id=1, source_target_pairs={{0,56},{8,0},{16,8},{24,16},{32,24},{40,32},{48,40},{56,48},{1,57}... | collective-permute-start | bytes 2359304 | tf_op jit(solution)/shard_map/ppermute | solution.py:23
  74.5 0.9 copy-start.13
  75.4 4.9 %copy-start.8 = (bf16[8,4,3,2,32,128]{5,4,3,2,1,0:T(8,128)(2,1)S(1)}, bf16[8,4,3,2,32,128]{5,4,3,2,1,0:T(8,128)(2,1)}, u32[]{:S(2)}) copy-start(bf16[8,4,3,2,32,128]{5,4,3,2,1,0:T(8,128)(2,1)} %shard_map.86.refs_2_.refs_15_) | copy-start | bytes 4718596
  77.5 11.5 %collective-permute-start.16 = (bf16[2,6,128,128]{3,2,1,0:T(8,128)(2,1)S(1)}, bf16[2,6,128,128]{3,2,1,0:T(8,128)(2,1)}, u32[]{:S(2)}, u32[]{:S(2)}) collective-permute-start(bf16[2,6,128,128]{3,2,1,0:T(8,128)(2,1)S(1)} %slice.6), channel_id=1, source_target_pairs={{0,8},{8,16},{16,24},{24,32},{32,40},{40,48},{48,56},{56,0},{1,9},... | collective-permute-start | bytes 1179656 | tf_op jit(solution)/shard_map/ppermute | solution.py:23
  77.6 11.4 %collective-permute-start.17 = (bf16[2,6,128,128]{3,2,1,0:T(8,128)(2,1)S(1)}, bf16[2,6,128,128]{3,2,1,0:T(8,128)(2,1)}, u32[]{:S(2)}, u32[]{:S(2)}) collective-permute-start(bf16[2,6,128,128]{3,2,1,0:T(8,128)(2,1)S(1)} %slice.7), channel_id=1, source_target_pairs={{0,56},{8,0},{16,8},{24,16},{32,24},{40,32},{48,40},{56,48},{1,57}... | collective-permute-start | bytes 1179656 | tf_op jit(solution)/shard_map/ppermute | solution.py:23
  81.5 1.5 copy-start.7
  83.0 27.5 %all-to-all-start.2 = ((bf16[32,3,2,32,128]{4,3,2,1,0:T(8,128)(2,1)}), bf16[32,3,2,32,128]{4,3,2,1,0:T(8,128)(2,1)S(1)}, u32[]{:S(2)}, u32[]{:S(2)}) async-start(bf16[32,3,2,32,128]{4,3,2,1,0:T(8,128)(2,1)} %bitcast.13), calls=%async_computation.2 | async-start | bytes 3145728 | tf_op jit(solution)/shard_map/all_to_all | solution.py:273
  110.5 39.1 %copy-start.2 = (s32[384]{0:T(512)S(1)}, s32[384]{0:T(512)}, u32[]{:S(2)}) copy-start(s32[384]{0:T(512)} %right_dims.3) | copy-start | bytes 4612
  110.5 39.1 %copy-start.4 = (s32[4]{0:T(128)S(1)}, s32[4]{0:T(128)}, u32[]{:S(2)}) copy-start(s32[4]{0:T(128)} %copy-done.3) | copy-start | bytes 52
  110.5 39.1 %copy-start.6 = (s32[8]{0:T(128)S(1)}, s32[8]{0:T(128)}, u32[]{:S(2)}) copy-start(s32[8]{0:T(128)} %constant.95.clone.place) | copy-start | bytes 100
